TPU v7x, 512 devices: a whole 4x8x8 slice. The times are simulated.
512 devices in a mesh: tm: 32 (over z, x), rows: 16 (over y, core).
Axes of the slice: x: 4, y: 8, z: 8, core: 2. Of those that a mesh axis runs over, the one named last changes fastest.
Arguments:
- frames: bfloat16 [64, 128, 48, 128], P('tm', 'rows'), may hold values from -60 to 60
- lengths: int32 [8], replicated, may hold values from 1 to 16, as said below
- norm_gain_one: float32 [128], replicated, may hold values from 0.5 to 1.5
- norm_shift_one: float32 [128], replicated, may hold values from -0.5 to 0.5
- conv_one: bfloat16 [3, 3, 3, 128, 128], replicated, may hold values from -0.109375 to 0.109375
- bias_one: float32 [128], replicated, may hold values from -1 to 1
- norm_gain_two: float32 [128], replicated, may hold values from 0.5 to 1.5
- norm_shift_two: float32 [128], replicated, may hold values from -0.5 to 0.5
- conv_two: bfloat16 [3, 3, 3, 128, 128], replicated, may hold values from -0.109375 to 0.109375
- bias_two: float32 [128], replicated, may hold values from -1 to 1
Outputs:
- encoded: float32 [64, 128, 48, 128], P('tm', 'rows')
Inputs may be any that keep to these rules, and one draw needn't show every extreme that they name: 8 video lengths that sum to 64; the longest has exactly 16 frames.
All inputs are finite; a program needn't handle non-finite values.
Results may differ from a plain program's by a relative error of at most 0.0014.
Values may be sent and summed in bfloat16 or wider, within the bound.
A program may use at most 64 MiB of HBM per device.

v0:
```python
import jax
import jax.numpy as jnp
from jax import lax
from jax.sharding import PartitionSpec as P

GROUPS = 32


def shifted(block, axis, distance):
    devices = range(lax.axis_size(axis))
    route = [(i - distance, i) for i in devices if i - distance in devices]
    return lax.ppermute(block, axis, route)


def extended(cells, sides, width):
    for axis, dim in sides:
        count = lax.axis_size(axis)
        ends = count - 1
        head = lax.slice_in_dim(cells, 0, width, axis=dim)
        tail = lax.slice_in_dim(cells, cells.shape[dim] - width, cells.shape[dim], axis=dim)
        cells = jnp.concatenate(
            [
                lax.ppermute(tail, axis, [(i, (i + 1) % count) for i in range(ends)]),
                cells,
                lax.ppermute(head, axis, [((i + 1) % count, i) for i in range(ends)]),
            ],
            axis=dim,
        )
    return cells


def plan_frames(lengths, count, first):
    videos = lengths.shape[0]
    offsets = jnp.cumsum(lengths) - lengths
    frame_ids = first + jnp.arange(count, dtype=jnp.int32)
    inside = offsets[None, :] <= frame_ids[:, None]
    video = jnp.sum(inside.astype(jnp.int32), axis=1) - 1
    starts = jnp.max(jnp.where(inside, offsets[None, :], 0), axis=1)
    onehot = (video[:, None] == jnp.arange(videos, dtype=jnp.int32)[None, :]).astype(jnp.float32)
    taps = [jnp.maximum(frame_ids - back, starts) - first + 2 for back in (2, 1, 0)]
    return (onehot, taps)


def group_totals(values):
    count = values.shape[0]
    width = values.shape[3]
    return jnp.sum(values, axis=(1, 2)).reshape(count, GROUPS, width // GROUPS).sum(-1)


def spread_groups(table, onehot, width):
    return jnp.repeat(
        jnp.dot(onehot, table, precision=lax.Precision.HIGHEST), width // GROUPS, axis=1
    )


def group_norm(values, onehot, counts, gain, shift):
    width = values.shape[3]
    sums = jnp.dot(onehot.T, group_totals(values), precision=lax.Precision.HIGHEST)
    mean = lax.psum(sums, ("tm", "rows")) / counts[:, None]
    centered = values - spread_groups(mean, onehot, width)[:, None, None, :]
    squares = jnp.dot(onehot.T, group_totals(centered * centered), precision=lax.Precision.HIGHEST)
    var = lax.psum(squares, ("tm", "rows")) / counts[:, None]
    scale = spread_groups(lax.rsqrt(var + 1e-06), onehot, width)
    return centered * scale[:, None, None, :] * gain + shift


def causal_conv(act, weight, bias, taps):
    count, height, cols_n, width = act.shape
    prior = shifted(act, "tm", 1)
    joined = jnp.concatenate([prior, act], axis=0)
    rimmed = extended(joined, (("rows", 1),), 1)
    padded = jnp.pad(rimmed, ((0, 0), (0, 0), (1, 1), (0, 0)))
    columns = jnp.concatenate(
        [padded[:, :, shift_col : shift_col + cols_n] for shift_col in range(3)], axis=-1
    )
    total = jnp.zeros((count * height * cols_n, width), jnp.float32)
    for step in range(3):
        picked = jnp.take(columns, taps[step], axis=0)
        for row_off in range(3):
            slab = picked[:, row_off : row_off + height].reshape(count * height * cols_n, 3 * width)
            kernel = weight[step, row_off].reshape(3 * width, width)
            total = total + jnp.dot(slab, kernel, preferred_element_type=jnp.float32)
    return total.reshape(count, height, cols_n, width) + bias


def per_device(
    frames,
    lengths,
    norm_gain_one,
    norm_shift_one,
    conv_one,
    bias_one,
    norm_gain_two,
    norm_shift_two,
    conv_two,
    bias_two,
):
    count, height, cols_n, width = frames.shape
    first = lax.axis_index("tm") * count
    onehot, taps = plan_frames(lengths, count, first)
    full_height = height * lax.axis_size("rows")
    counts = lengths.astype(jnp.float32) * (full_height * cols_n * (width // GROUPS))
    values = frames.astype(jnp.float32)
    act_one = jax.nn.silu(group_norm(values, onehot, counts, norm_gain_one, norm_shift_one)).astype(
        jnp.bfloat16
    )
    middle = causal_conv(act_one, conv_one, bias_one, taps).astype(jnp.bfloat16)
    act_two = jax.nn.silu(
        group_norm(middle.astype(jnp.float32), onehot, counts, norm_gain_two, norm_shift_two)
    ).astype(jnp.bfloat16)
    return values + causal_conv(act_two, conv_two, bias_two, taps)


def solution(mesh):
    placed = (P("tm", "rows", None, None), P(), P(), P(), P(), P(), P(), P(), P(), P())
    return jax.shard_map(
        per_device,
        mesh=mesh,
        in_specs=placed,
        out_specs=P("tm", "rows", None, None),
        check_vma=False,
    )
```

profile of v0, /device:TPU:89, one launch (start us, length us, event | category | flops | bytes accessed | tf_op | source)
XLA Modules:
  0.0 459.6 jit_solution(9391679192439192227)
XLA Ops:
  0.0 0.7 convert_multiply_fusion
  0.7 0.8 reduce-window.9
  1.6 0.7 bitcast_subtract_fusion
  2.4 1.0 convert_reduce_fusion
  3.9 101.7 %psum.28 = f32[8,32]{1,0:T(8,128)S(1)} all-reduce(f32[8,32]{1,0:T(8,128)S(1)} %fusion.56), channel_id=1, replica_groups=mesh['tm'=32,'rows'=16] {'tm','rows'}, use_global_device_ids=true, to_apply=%region_4.5 | all-reduce | flops 256 | bytes 2048 | tf_op jit(solution)/shard_map/psum | solution.py:59
  106.0 1.0 fusion.15
  107.5 94.3 %psum.29 = f32[8,32]{1,0:T(8,128)S(1)} all-reduce(f32[8,32]{1,0:T(8,128)S(1)} %fusion.55), channel_id=1, replica_groups=mesh['tm'=32,'rows'=16] {'tm','rows'}, use_global_device_ids=true, to_apply=%region_7.8 | all-reduce | flops 256 | bytes 2048 | tf_op jit(solution)/shard_map/psum | solution.py:62
  202.2 1.1 fusion.23
  203.3 3.7 collective-permute-start
  207.1 1.0 fusion.68
  208.1 5.6 %collective-permute-done = bf16[2,8,48,128]{3,2,1,0:T(8,128)(2,1)S(1)} collective-permute-done((bf16[2,8,48,128]{3,2,1,0:T(8,128)(2,1)S(1)}, bf16[2,8,48,128]{3,2,1,0:T(8,128)(2,1)S(1)}, u32[]{:S(2)}, u32[]{:S(2)}) %collective-permute-start) | collective-permute-done | bytes 196640 | tf_op jit(solution)/shard_map/ppermute | solution.py:12
  213.7 5.1 %collective-permute-start.1 = (bf16[4,1,48,128]{3,2,1,0:T(8,128)(2,1)S(1)}, bf16[4,1,48,128]{3,2,1,0:T(8,128)(2,1)S(1)}, u32[]{:S(2)}, u32[]{:S(2)}) collective-permute-start(bf16[4,1,48,128]{3,2,1,0:T(8,128)(2,1)S(1)} %get-tuple-element.58), channel_id=1, source_target_pairs={{0,1},{1,2},{2,3},{3,4},{4,5},{5,6},{6,7},{7,8},{8,9},{9,10},{10,1... | collective-permute-start | bytes 147464 | tf_op jit(solution)/shard_map/ppermute | solution.py:23
  218.8 1.9 collective-permute-start.2
  220.8 4.7 %collective-permute-done.2 = bf16[4,1,48,128]{3,2,1,0:T(8,128)(2,1)S(1)} collective-permute-done((bf16[4,1,48,128]{3,2,1,0:T(8,128)(2,1)S(1)}, bf16[4,1,48,128]{3,2,1,0:T(8,128)(2,1)S(1)}, u32[]{:S(2)}, u32[]{:S(2)}) %collective-permute-start.2) | collective-permute-done | bytes 49184 | tf_op jit(solution)/shard_map/ppermute | solution.py:25
  226.2 0.7 gather_fusion.2
  226.9 1.5 gather_fusion
  228.4 1.3 broadcast_select_fusion
  229.8 1.2 fusion.74
  231.0 0.7 gather_fusion.1
  232.2 0.7 copy-done.13
  232.9 0.3 fusion.77
  233.6 0.3 convolution_add_fusion.14
  234.2 0.3 convolution_add_fusion.13
  234.5 0.3 convolution_add_fusion.12
  235.4 0.3 convolution_add_fusion.10
  236.4 0.3 convolution_add_fusion.8
  237.2 94.4 %psum.30 = f32[8,32]{1,0:T(8,128)S(1)} all-reduce(f32[8,32]{1,0:T(8,128)S(1)} %fusion.54), channel_id=1, replica_groups=mesh['tm'=32,'rows'=16] {'tm','rows'}, use_global_device_ids=true, to_apply=%region_11.13 | all-reduce | flops 256 | bytes 2048 | tf_op jit(solution)/shard_map/psum | solution.py:59
  332.6 94.1 %psum.31 = f32[8,32]{1,0:T(8,128)S(1)} all-reduce(f32[8,32]{1,0:T(8,128)S(1)} %fusion.53), channel_id=1, replica_groups=mesh['tm'=32,'rows'=16] {'tm','rows'}, use_global_device_ids=true, to_apply=%region_14.16 | all-reduce | flops 256 | bytes 2048 | tf_op jit(solution)/shard_map/psum | solution.py:62
  427.2 2.8 collective-permute-start.3
  430.0 7.0 %collective-permute-done.3 = bf16[2,8,48,128]{3,2,1,0:T(8,128)(2,1)S(1)} collective-permute-done((bf16[2,8,48,128]{3,2,1,0:T(8,128)(2,1)S(1)}, bf16[2,8,48,128]{3,2,1,0:T(8,128)(2,1)S(1)}, u32[]{:S(2)}, u32[]{:S(2)}) %collective-permute-start.3) | collective-permute-done | bytes 196640 | tf_op jit(solution)/shard_map/ppermute | solution.py:12
  437.0 5.1 %collective-permute-start.4 = (bf16[4,1,48,128]{3,2,1,0:T(8,128)(2,1)S(1)}, bf16[4,1,48,128]{3,2,1,0:T(8,128)(2,1)S(1)}, u32[]{:S(2)}, u32[]{:S(2)}) collective-permute-start(bf16[4,1,48,128]{3,2,1,0:T(8,128)(2,1)S(1)} %get-tuple-element.56), channel_id=1, source_target_pairs={{0,1},{1,2},{2,3},{3,4},{4,5},{5,6},{6,7},{7,8},{8,9},{9,10},{10,1... | collective-permute-start | bytes 147464 | tf_op jit(solution)/shard_map/ppermute | solution.py:23
  442.1 2.1 collective-permute-start.5
  444.2 0.8 fusion.67
  444.9 3.7 collective-permute-done.5
  449.4 1.5 gather_fusion.3
  450.9 0.7 gather_fusion.4
  451.6 0.7 gather_fusion.5
  452.4 1.3 broadcast_select_fusion.1
  454.1 0.4 copy-done.18
  454.9 0.7 copy-done.16
  455.6 0.3 fusion.78
  456.6 0.3 convolution_add_fusion.5
  456.9 0.3 convolution_add_fusion.4
  457.3 0.3 convolution_add_fusion.3
  457.6 0.3 convolution_add_fusion.2
  457.9 0.3 convolution_add_fusion.1
  458.3 0.3 convolution_add_fusion
  458.8 0.8 convert_add_fusion
  (112 shorter events, 9.2 us)
Async XLA Ops:
  0.0 207.1 %copy-start.3 = (bf16[3,3,3,128,128]{4,3,2,1,0:T(8,128)(2,1)S(1)}, bf16[3,3,3,128,128]{4,3,2,1,0:T(8,128)(2,1)}, u32[]{:S(2)}) copy-start(bf16[3,3,3,128,128]{4,3,2,1,0:T(8,128)(2,1)} %param.16) | copy-start | bytes 2654212
  0.7 207.3 %copy-start.25 = (f32[8]{0:T(128)}, f32[8]{0:T(128)S(1)}, u32[]{:S(2)}) copy-start(f32[8]{0:T(128)S(1)} %convert_multiply_fusion) | copy-start | bytes 100
  2.4 205.6 %copy-start.27 = (s32[2]{0:T(128)}, s32[2]{0:T(128)S(1)}, u32[]{:S(2)}) copy-start(s32[2]{0:T(128)S(1)} %broadcast_add_fusion) | copy-start | bytes 28
  203.3 10.4 %collective-permute-start = (bf16[2,8,48,128]{3,2,1,0:T(8,128)(2,1)S(1)}, bf16[2,8,48,128]{3,2,1,0:T(8,128)(2,1)S(1)}, u32[]{:S(2)}, u32[]{:S(2)}) collective-permute-start(bf16[2,8,48,128]{3,2,1,0:T(8,128)(2,1)S(1)} %fusion.23), channel_id=1, source_target_pairs={{0,16},{16,32},{32,48},{48,64},{64,80},{80,96},{96,112},{112,128},... | collective-permute-start | bytes 589832 | tf_op jit(solution)/shard_map/ppermute | solution.py:12
  207.0 21.4 %copy-start.17 = (pred[2]{0:T(512)(128)(4,1)}, pred[2]{0:T(512)(128)(4,1)S(1)}, u32[]{:S(2)}) copy-start(pred[2]{0:T(512)(128)(4,1)S(1)} %get-tuple-element.10) | copy-start | bytes 10
  207.0 21.4 %copy-start.19 = (pred[2]{0:T(512)(128)(4,1)}, pred[2]{0:T(512)(128)(4,1)S(1)}, u32[]{:S(2)}) copy-start(pred[2]{0:T(512)(128)(4,1)S(1)} %get-tuple-element.62) | copy-start | bytes 10
  213.7 7.1 %collective-permute-start.1 = (bf16[4,1,48,128]{3,2,1,0:T(8,128)(2,1)S(1)}, bf16[4,1,48,128]{3,2,1,0:T(8,128)(2,1)S(1)}, u32[]{:S(2)}, u32[]{:S(2)}) collective-permute-start(bf16[4,1,48,128]{3,2,1,0:T(8,128)(2,1)S(1)} %get-tuple-element.58), channel_id=1, source_target_pairs={{0,1},{1,2},{2,3},{3,4},{4,5},{5,6},{6,7},{7,8},{8,9},{9,10},{10,1... | collective-permute-start | bytes 147464 | tf_op jit(solution)/shard_map/ppermute | solution.py:23
  218.8 6.6 %collective-permute-start.2 = (bf16[4,1,48,128]{3,2,1,0:T(8,128)(2,1)S(1)}, bf16[4,1,48,128]{3,2,1,0:T(8,128)(2,1)S(1)}, u32[]{:S(2)}, u32[]{:S(2)}) collective-permute-start(bf16[4,1,48,128]{3,2,1,0:T(8,128)(2,1)S(1)} %get-tuple-element.59), channel_id=1, source_target_pairs={{1,0},{2,1},{3,2},{4,3},{5,4},{6,5},{7,6},{8,7},{9,8},{10,9},{11,1... | collective-permute-start | bytes 147464 | tf_op jit(solution)/shard_map/ppermute | solution.py:25
  232.0 0.9 copy-start.13
  232.0 1.2 copy-start.2
  232.0 1.2 copy-start.12
  232.2 1.4 copy-start.1
  232.2 1.4 copy-start.11
  233.3 0.9 copy-start.10
  233.6 0.9 copy-start.9
  234.2 0.9 copy-start.8
  234.5 0.9 copy-start.7
  235.1 0.9 copy-start.6
  235.4 0.9 copy-start.5
  236.0 0.7 copy-start.24
  236.0 1.0 copy-start.28
  236.3 95.3 %copy-start.26 = (f32[8]{0:T(128)S(1)}, f32[8]{0:T(128)}, u32[]{:S(2)}) copy-start(f32[8]{0:T(128)} %copy-done.25) | copy-start | bytes 100
  236.3 190.7 %copy-start.22 = (f32[128]{0:T(128)S(1)}, f32[128]{0:T(128)}, u32[]{:S(2)}) copy-start(f32[128]{0:T(128)} %param.19) | copy-start | bytes 1540
  236.3 190.7 %copy-start.23 = (f32[128]{0:T(128)S(1)}, f32[128]{0:T(128)}, u32[]{:S(2)}) copy-start(f32[128]{0:T(128)} %param.18) | copy-start | bytes 1540
  236.7 207.5 %copy-start.4 = (bf16[3,3,3,128,128]{4,3,2,1,0:T(8,128)(2,1)S(1)}, bf16[3,3,3,128,128]{4,3,2,1,0:T(8,128)(2,1)}, u32[]{:S(2)}) copy-start(bf16[3,3,3,128,128]{4,3,2,1,0:T(8,128)(2,1)} %param.20) | copy-start | bytes 2654212
  427.2 9.8 %collective-permute-start.3 = (bf16[2,8,48,128]{3,2,1,0:T(8,128)(2,1)S(1)}, bf16[2,8,48,128]{3,2,1,0:T(8,128)(2,1)S(1)}, u32[]{:S(2)}, u32[]{:S(2)}) collective-permute-start(bf16[2,8,48,128]{3,2,1,0:T(8,128)(2,1)S(1)} %fusion.32), channel_id=1, source_target_pairs={{0,16},{16,32},{32,48},{48,64},{64,80},{80,96},{96,112},{112,128},... | collective-permute-start | bytes 589832 | tf_op jit(solution)/shard_map/ppermute | solution.py:12
  437.0 8.0 %collective-permute-start.4 = (bf16[4,1,48,128]{3,2,1,0:T(8,128)(2,1)S(1)}, bf16[4,1,48,128]{3,2,1,0:T(8,128)(2,1)S(1)}, u32[]{:S(2)}, u32[]{:S(2)}) collective-permute-start(bf16[4,1,48,128]{3,2,1,0:T(8,128)(2,1)S(1)} %get-tuple-element.56), channel_id=1, source_target_pairs={{0,1},{1,2},{2,3},{3,4},{4,5},{5,6},{6,7},{7,8},{8,9},{9,10},{10,1... | collective-permute-start | bytes 147464 | tf_op jit(solution)/shard_map/ppermute | solution.py:23
  442.1 6.6 %collective-permute-start.5 = (bf16[4,1,48,128]{3,2,1,0:T(8,128)(2,1)S(1)}, bf16[4,1,48,128]{3,2,1,0:T(8,128)(2,1)S(1)}, u32[]{:S(2)}, u32[]{:S(2)}) collective-permute-start(bf16[4,1,48,128]{3,2,1,0:T(8,128)(2,1)S(1)} %get-tuple-element.57), channel_id=1, source_target_pairs={{1,0},{2,1},{3,2},{4,3},{5,4},{6,5},{7,6},{8,7},{9,8},{10,9},{11,1... | collective-permute-start | bytes 147464 | tf_op jit(solution)/shard_map/ppermute | solution.py:25
  450.9 1.4 copy-start.20
  454.0 0.6 copy-start.18
  454.7 0.9 copy-start.16
  454.7 1.2 copy-start.15
  454.9 1.4 copy-start.14
  457.9 0.9 copy-start
  457.9 0.9 copy-start.21
where the time goes:
time: 460 us
  blocking collectives  385 us (84%)
  waiting for transfers between devices  21 us (5%)
  starting transfers between devices  20.7 us (4%)
  local copies, waits for them, and re-layouts  14.3 us (3%)
  other arithmetic  11 us (2%)
  matrix products  7.45 us (2%)
    psum x2, blocking collectives, group_norm(): mean = lax.psum(sums, ('tm', 'rows')) / counts[:, None]  196 us
    psum x2, blocking collectives, group_norm(): var = lax.psum(squares, ('tm', 'rows')) / counts[:, None]  188 us
    ppermute x2, waiting for transfers between devices, shifted(): return lax.ppermute(block, axis, route)  12.6 us
    ppermute x2, starting transfers between devices, extended(): lax.ppermute(tail, axis, [(i, (i + 1) % count) for i in range(ends)])  10.2 us
  transfers between devices with their start and end apart: 6, of which 4 were waited for; matrix products, arithmetic and copies ran while one was open for 0% of the time, Pallas kernels for 0%

commit v1 on v0

v1 whole, which is shorter than its diff:
```python
import functools

import jax
import jax.numpy as jnp
from jax import lax
from jax.experimental import pallas as pl
from jax.experimental.pallas import tpu as pltpu
from jax.sharding import PartitionSpec as P

GROUPS = 32
MOST = 16
MESH = pl.DeviceIdType.MESH


def tm_offsets(n_tm, count):
    reach = -(-(MOST - 1) // count)
    if 2 * reach + 1 >= n_tm:
        return list(range(n_tm))
    return list(range(reach + 1)) + [-d for d in range(1, reach + 1)]


def wrapped(index, offset, size):
    return lax.rem(index + (offset + size), size)


def group_total(row, width):
    lane = lax.broadcasted_iota(jnp.int32, row.shape, 1)
    channels = row.shape[1]
    span = 1
    while span < width:
        ahead = pltpu.roll(row, channels - span, 1)
        behind = pltpu.roll(row, span, 1)
        row = row + jnp.where((lane // span) % 2 == 0, ahead, behind)
        span *= 2
    return row


def kernel(
    n_tm, n_rows,
    frames, lengths, gain_one, shift_one, conv_one, bias_one, gain_two, shift_two, conv_two, bias_two,
    out,
    raw, mid, act, taps_one, taps_two, vecs, lens, rows_one, rows_two, tms_one, tms_two, result,
    load_sem, halo_send, halo_recv, stat_send, stat_recv, out_sem,
):
    count, height, cols, width = frames.shape
    videos = lengths.shape[0]
    tm = lax.axis_index("tm")
    row = lax.axis_index("rows")
    first = tm * count
    offsets = tm_offsets(n_tm, count)

    load_frames = pltpu.make_async_copy(
        frames, raw.at[pl.ds(count, count), pl.ds(1, height)], load_sem.at[0]
    )
    load_frames.start()
    load_lens = pltpu.make_async_copy(lengths, lens, load_sem.at[1])
    load_lens.start()
    load_vecs = []
    for i, vec in enumerate((gain_one, shift_one, bias_one, gain_two, shift_two, bias_two)):
        load_vecs.append(pltpu.make_async_copy(vec, vecs.at[i], load_sem.at[2 + i]))
    load_one, load_two = [], []
    for dx in range(3):
        load_one.append(
            pltpu.make_async_copy(
                conv_one.at[:, :, dx], taps_one.at[:, :, :, pl.ds(dx * width, width)], load_sem.at[8 + dx]
            )
        )
        load_two.append(
            pltpu.make_async_copy(
                conv_two.at[:, :, dx], taps_two.at[:, :, :, pl.ds(dx * width, width)], load_sem.at[11 + dx]
            )
        )

    peers = [(0, k) for k in range(1, n_rows)]
    peers += [(d, 0) for d in offsets[1:]]
    peers += [(d, k) for d in (1, -1) for k in (1, -1)]
    barrier = pltpu.get_barrier_semaphore()
    for d, k in peers:
        pl.semaphore_signal(
            barrier,
            inc=1,
            device_id={"tm": wrapped(tm, d, n_tm), "rows": wrapped(row, k, n_rows)},
            device_id_type=MESH,
        )
    for load in load_vecs + load_one + load_two:
        load.start()

    def halo_copies(block, half):
        own = pl.ds(count, count)
        prior = pl.ds(0, count)
        plans = [
            (block.at[own, pl.ds(1, height)], block.at[prior, pl.ds(1, height)], 1, 0),
            (block.at[own, pl.ds(height, 1)], block.at[own, pl.ds(0, 1)], 0, 1),
            (block.at[own, pl.ds(1, 1)], block.at[own, pl.ds(height + 1, 1)], 0, -1),
            (block.at[own, pl.ds(height, 1)], block.at[prior, pl.ds(0, 1)], 1, 1),
            (block.at[own, pl.ds(1, 1)], block.at[prior, pl.ds(height + 1, 1)], 1, -1),
        ]
        return [
            pltpu.make_async_remote_copy(
                src_ref=src,
                dst_ref=dst,
                send_sem=halo_send.at[half, i],
                recv_sem=halo_recv.at[half, i],
                device_id={"tm": wrapped(tm, d, n_tm), "rows": wrapped(row, k, n_rows)},
                device_id_type=MESH,
            )
            for i, (src, dst, d, k) in enumerate(plans)
        ]

    def spread(slots, steps, sem):
        for i, (d, k) in enumerate(steps):
            pltpu.make_async_remote_copy(
                src_ref=slots.at[0],
                dst_ref=slots.at[1 + i],
                send_sem=stat_send.at[sem],
                recv_sem=stat_recv.at[sem],
                device_id={"tm": wrapped(tm, d, n_tm), "rows": wrapped(row, k, n_rows)},
                device_id_type=MESH,
            ).start()

    def whole(slots, steps, sem):
        others = slots.at[pl.ds(1, len(steps))]
        return pltpu.make_async_remote_copy(
            src_ref=others,
            dst_ref=others,
            send_sem=stat_send.at[sem],
            recv_sem=stat_recv.at[sem],
            device_id={"tm": wrapped(tm, 1, n_tm), "rows": row},
            device_id_type=MESH,
        )

    row_steps = [(0, k) for k in range(1, n_rows)]
    tm_steps = [(d, 0) for d in offsets[1:]]
    per_block = float(height * cols)
    per_frame = per_block * n_rows

    def local_stats(block):
        sums, squares = [], []
        for f in range(count):
            values = block[count + f, 1 : height + 1].reshape(height * cols, width).astype(jnp.float32)
            total = jnp.sum(values, axis=0, keepdims=True)
            off = values - total * (1.0 / per_block)
            sums.append(total)
            squares.append(jnp.sum(off * off, axis=0, keepdims=True))
        return jnp.concatenate(sums + squares + [jnp.zeros((8 - 2 * count, width), jnp.float32)], axis=0)

    def merged_rows(slots):
        parts = slots[...]
        total = jnp.sum(parts, axis=0)
        off = parts * (1.0 / per_block) - (total * (1.0 / per_frame))[None]
        between = jnp.sum(off * off, axis=0) * per_block
        return jnp.concatenate(
            [
                total[:count],
                total[count : 2 * count] + between[:count],
                jnp.zeros((8 - 2 * count, width), jnp.float32),
            ],
            axis=0,
        )

    def merged_frames(slots, inside, length):
        parts = slots[...]
        total = jnp.sum(jnp.where(inside, parts, 0.0), axis=0)
        entries = length.astype(jnp.float32) * (per_frame * (width // GROUPS))
        mean = group_total(jnp.sum(total[:count], axis=0, keepdims=True), width // GROUPS) / entries
        off = parts * (1.0 / per_frame) - mean[None]
        between = jnp.sum(jnp.where(inside, off * off, 0.0), axis=0) * per_frame
        squares = jnp.sum(total[count : 2 * count] + between[:count], axis=0, keepdims=True)
        var = group_total(squares, width // GROUPS) / entries
        return mean, lax.rsqrt(var + 1e-6)

    def activate(block, stats, gain, shift):
        top = row == 0
        bottom = row == n_rows - 1
        for f in range(2 * count):
            mean, scale = stats[max(f - count, 0)]
            factor = scale * gain
            for i in range(height + 2):
                v = (block[f, i].astype(jnp.float32) - mean) * factor + shift
                v = v * (0.5 * jnp.tanh(0.5 * v) + 0.5)
                if i == 0:
                    v = jnp.where(top, 0.0, v)
                if i == height + 1:
                    v = jnp.where(bottom, 0.0, v)
                act[f, i] = v.astype(jnp.bfloat16)

    def conv(taps, sources):
        lefts = []
        for f in range(count):
            pieces = []
            for dt in range(3):
                for dy in range(3):
                    pieces.append(
                        act[sources[f][dt], dy : dy + height].reshape(height * cols, width)
                    )
            lefts.append(jnp.concatenate(pieces, axis=1))
        left = jnp.concatenate(lefts, axis=0)
        right = taps[...].reshape(9 * width, 3 * width)
        return jnp.dot(left, right, preferred_element_type=jnp.float32)

    column = lax.broadcasted_iota(jnp.int32, (cols, width), 0)

    def joined(wide, i):
        y = wide[i * cols : (i + 1) * cols]
        before = pltpu.roll(y[:, :width], 1, 0)
        after = pltpu.roll(y[:, 2 * width :], cols - 1, 0)
        return (
            y[:, width : 2 * width]
            + jnp.where(column == 0, 0.0, before)
            + jnp.where(column == cols - 1, 0.0, after)
        )

    load_frames.wait()
    rows_one[0] = local_stats(raw)
    pl.semaphore_wait(barrier, len(peers))
    spread(rows_one, row_steps, 0)
    halo_one = halo_copies(raw, 0)
    for copy in halo_one:
        copy.start()

    load_lens.wait()
    starts, stops = [], []
    for f in range(count):
        start = jnp.int32(0)
        stop = jnp.int32(0)
        offset = jnp.int32(0)
        for v in range(videos):
            size = lens[v]
            here = offset <= first + f
            start = jnp.where(here, offset, start)
            stop = jnp.where(here, offset + size, stop)
            offset = offset + size
        starts.append(start)
        stops.append(stop)
    slot = lax.broadcasted_iota(jnp.int32, tms_one.shape, 0)
    part = lax.broadcasted_iota(jnp.int32, tms_one.shape, 1)
    reach = max(offsets)
    base = first - count * jnp.where(slot <= reach, slot, reach - slot)
    base = jnp.where(base < 0, base + count * n_tm, base)
    base = jnp.where(base >= count * n_tm, base - count * n_tm, base)
    frame = base + lax.rem(part, count)
    inside = [(frame >= starts[f]) & (frame < stops[f]) for f in range(count)]
    sources = [
        [jnp.maximum(f + dt, starts[f] - first + 2) for dt in range(3)] for f in range(count)
    ]

    whole(rows_one, row_steps, 0).wait_recv()
    tms_one[0] = merged_rows(rows_one)
    spread(tms_one, tm_steps, 1)
    for load in load_vecs:
        load.wait()
    whole(tms_one, tm_steps, 1).wait_recv()
    stats = [merged_frames(tms_one, inside[f], stops[f] - starts[f]) for f in range(count)]
    for copy in halo_one:
        copy.wait_recv()
    activate(raw, stats, vecs[0:1], vecs[1:2])
    for load in load_one:
        load.wait()
    wide = conv(taps_one, sources)
    for f in range(count):
        for i in range(height):
            mid[count + f, 1 + i] = (joined(wide, f * height + i) + vecs[2:3]).astype(jnp.bfloat16)

    rows_two[0] = local_stats(mid)
    spread(rows_two, row_steps, 2)
    halo_two = halo_copies(mid, 1)
    for copy in halo_two:
        copy.start()
    whole(rows_two, row_steps, 2).wait_recv()
    tms_two[0] = merged_rows(rows_two)
    spread(tms_two, tm_steps, 3)
    whole(tms_two, tm_steps, 3).wait_recv()
    stats = [merged_frames(tms_two, inside[f], stops[f] - starts[f]) for f in range(count)]
    for copy in halo_two:
        copy.wait_recv()
    activate(mid, stats, vecs[3:4], vecs[4:5])
    for load in load_two:
        load.wait()
    wide = conv(taps_two, sources)
    stores = []
    for f in range(count):
        for i in range(height):
            result[f, i] = (
                joined(wide, f * height + i) + vecs[5:6] + raw[count + f, 1 + i].astype(jnp.float32)
            )
        stores.append(pltpu.make_async_copy(result.at[f], out.at[f], out_sem.at[f]))
        stores[-1].start()

    for copy in halo_one + halo_two:
        copy.wait_send()
    whole(rows_one, row_steps, 0).wait_send()
    whole(tms_one, tm_steps, 1).wait_send()
    whole(rows_two, row_steps, 2).wait_send()
    whole(tms_two, tm_steps, 3).wait_send()
    for store in stores:
        store.wait()


def per_device(n_tm, n_rows, *args):
    frames, lengths = args[0], args[1]
    count, height, cols, width = frames.shape
    window = len(tm_offsets(n_tm, count))
    block = pltpu.VMEM((2 * count, height + 2, cols, width), jnp.bfloat16)
    taps = pltpu.VMEM((3, 3, width, 3 * width), jnp.bfloat16)
    return pl.pallas_call(
        functools.partial(kernel, n_tm, n_rows),
        out_shape=jax.ShapeDtypeStruct(frames.shape, jnp.float32),
        in_specs=[pl.BlockSpec(memory_space=pl.ANY)] * len(args),
        out_specs=pl.BlockSpec(memory_space=pl.ANY),
        scratch_shapes=[
            block, block, block, taps, taps,
            pltpu.VMEM((8, width), jnp.float32),
            pltpu.SMEM(lengths.shape, jnp.int32),
            pltpu.VMEM((n_rows, 8, width), jnp.float32),
            pltpu.VMEM((n_rows, 8, width), jnp.float32),
            pltpu.VMEM((window, 8, width), jnp.float32),
            pltpu.VMEM((window, 8, width), jnp.float32),
            pltpu.VMEM(frames.shape, jnp.float32),
            pltpu.SemaphoreType.DMA((14,)),
            pltpu.SemaphoreType.DMA((2, 5)),
            pltpu.SemaphoreType.DMA((2, 5)),
            pltpu.SemaphoreType.DMA((4,)),
            pltpu.SemaphoreType.DMA((4,)),
            pltpu.SemaphoreType.DMA((count,)),
        ],
        compiler_params=pltpu.CompilerParams(
            collective_id=0, has_side_effects=True, vmem_limit_bytes=63 * 1024 * 1024
        ),
        name="residual_block",
    )(*args)


def solution(mesh):
    placed = (P("tm", "rows", None, None), P(), P(), P(), P(), P(), P(), P(), P(), P())
    return jax.shard_map(
        functools.partial(per_device, mesh.shape["tm"], mesh.shape["rows"]),
        mesh=mesh,
        in_specs=placed,
        out_specs=P("tm", "rows", None, None),
        check_vma=False,
    )
```

time: 460 us -> 42.2 us (0.09)
  the two profiles are of different devices: /device:TPU:89 before, /device:TPU:1 now
where the time goes in v1:
time: 42.2 us; the launch traced here: 42 us
  Pallas kernels  40.3 us (95%)
  local copies, waits for them, and re-layouts  1.77 us (4%)
    pallas_call x1, Pallas kernels, per_device(): pl.pallas_call(functools.partial(kernel, n_tm, n_rows), out_shape=jax.Sha...  40.3 us
    unnamed x1, local copies, waits for them, and re-layouts  1.77 us

profile of v1, /device:TPU:1, one launch (start us, length us, event | category | flops | bytes accessed | tf_op | source)
XLA Modules:
  0.0 42.0 jit_solution(17350651194154710989)
XLA Ops:
  0.0 40.3 %residual_block.1 = f32[2,8,48,128]{3,2,1,0:T(8,128)} custom-call(bf16[2,8,48,128]{3,2,1,0:T(8,128)(2,1)} %frames.1, s32[8]{0:T(128)} %lengths.1, f32[128]{0:T(128)} %gain_one.1, f32[128]{0:T(128)} %shift_one.1, bf16[3,3,3,128,128]{4,3,2,1,0:T(8,128)(2,1)} %conv_one.1, f32[128]{0:T(128)} %bias_one.1, f32[128]{0:T(128)} %gain_two.1, f32[128]{0:T(128)} %shift_two.1, ...), custom_call_target="tpu_custom_call" | custom-call | tf_op jit(solution)/shard_map/residual_block/pallas_call | solution.py:305
  40.3 1.8 %copy.12 = f32[2,8,48,128]{3,2,1,0:T(8,128)} copy(f32[2,8,48,128]{3,2,1,0:T(8,128)} %residual_block.1) | data formatting | bytes 786432

commit v2 on v1

v2 whole, which is shorter than its diff:
```python
import functools

import jax
import jax.numpy as jnp
from jax import lax
from jax.experimental import pallas as pl
from jax.experimental.pallas import tpu as pltpu
from jax.sharding import PartitionSpec as P

GROUPS = 32
MOST = 16
MESH = pl.DeviceIdType.MESH


def tm_offsets(n_tm, count):
    reach = min(-(-(MOST - 1) // count), n_tm - 1)
    return [d for far in range(1, reach + 1) for d in (far, -far)]


def wrapped(index, offset, size):
    return lax.rem(index + (offset + size), size)


def group_total(row, width):
    lane = lax.broadcasted_iota(jnp.int32, row.shape, 1)
    channels = row.shape[1]
    span = 1
    while span < width:
        ahead = pltpu.roll(row, channels - span, 1)
        behind = pltpu.roll(row, span, 1)
        row = row + jnp.where((lane // span) % 2 == 0, ahead, behind)
        span *= 2
    return row


def kernel(
    n_tm, n_rows,
    frames, lengths, gain_one, shift_one, conv_one, bias_one, gain_two, shift_two, conv_two, bias_two,
    out,
    raw, mid, act, taps_one, taps_two, vecs, lens, rows_one, rows_two, tms_one, tms_two, result,
    load_sem, halo_send, halo_recv, row_send, row_recv, tm_send, tm_recv, out_sem,
):
    count, height, cols, width = frames.shape
    videos = lengths.shape[0]
    tm = lax.axis_index("tm")
    row = lax.axis_index("rows")
    first = tm * count
    offsets = tm_offsets(n_tm, count)

    load_frames = pltpu.make_async_copy(
        frames, raw.at[pl.ds(count, count), pl.ds(1, height)], load_sem.at[0]
    )
    load_frames.start()

    def exists(d):
        return (tm + d >= 0) & (tm + d < n_tm)

    def device(d, k):
        return {"tm": tm + d, "rows": wrapped(row, k, n_rows)}

    barrier = pltpu.get_barrier_semaphore()
    for k in range(1, n_rows):
        pl.semaphore_signal(barrier, inc=1, device_id=device(0, k), device_id_type=MESH)
    expected = n_rows - 1
    for d in sorted(offsets, key=abs, reverse=True):
        present = exists(d)
        steps = (0, 1, -1) if abs(d) == 1 else (0,)
        expected = expected + jnp.where(present, len(steps), 0)

        @pl.when(present)
        def _(d=d, steps=steps):
            for k in steps:
                pl.semaphore_signal(barrier, inc=1, device_id=device(d, k), device_id_type=MESH)

    load_lens = pltpu.make_async_copy(lengths, lens, load_sem.at[1])
    load_lens.start()
    load_vecs = []
    for i, vec in enumerate((gain_one, shift_one, bias_one, gain_two, shift_two, bias_two)):
        load_vecs.append(pltpu.make_async_copy(vec, vecs.at[i], load_sem.at[2 + i]))
    load_one, load_two = [], []
    for dx in range(3):
        load_one.append(
            pltpu.make_async_copy(
                conv_one.at[:, :, dx], taps_one.at[:, :, :, pl.ds(dx * width, width)], load_sem.at[8 + dx]
            )
        )
        load_two.append(
            pltpu.make_async_copy(
                conv_two.at[:, :, dx], taps_two.at[:, :, :, pl.ds(dx * width, width)], load_sem.at[11 + dx]
            )
        )
    for load in load_vecs + load_one + load_two:
        load.start()

    class Halo:
        def __init__(self, block, half):
            own, prior = pl.ds(count, count), pl.ds(0, count)
            whole, last, head = pl.ds(1, height), pl.ds(height, 1), pl.ds(1, 1)
            above, below = pl.ds(0, 1), pl.ds(height + 1, 1)
            plans = [
                (own, last, own, above, 0, 1),
                (own, head, own, below, 0, -1),
                (own, last, prior, above, 1, 1),
                (own, head, prior, below, 1, -1),
                (own, whole, prior, whole, 1, 0),
            ]
            copies = [
                pltpu.make_async_remote_copy(
                    src_ref=block.at[f, src],
                    dst_ref=block.at[g, dst],
                    send_sem=halo_send.at[half, i],
                    recv_sem=halo_recv.at[half, i],
                    device_id=device(d, k),
                    device_id_type=MESH,
                )
                for i, (f, src, g, dst, d, k) in enumerate(plans)
            ]
            self.beside, self.onward = copies[:2], copies[2:]

        def start(self):
            for copy in self.beside:
                copy.start()

            @pl.when(exists(1))
            def _():
                for copy in self.onward:
                    copy.start()

        def wait_recv(self):
            for copy in self.beside:
                copy.wait_recv()

            @pl.when(exists(-1))
            def _():
                for copy in self.onward:
                    copy.wait_recv()

        def wait_send(self):
            for copy in self.beside:
                copy.wait_send()

            @pl.when(exists(1))
            def _():
                for copy in self.onward:
                    copy.wait_send()

    class Rows:
        def __init__(self, slots, half):
            self.copies = [
                pltpu.make_async_remote_copy(
                    src_ref=slots.at[pl.ds(0, 1)],
                    dst_ref=slots.at[pl.ds(k, 1)],
                    send_sem=row_send.at[half, k],
                    recv_sem=row_recv.at[half, k],
                    device_id=device(0, k),
                    device_id_type=MESH,
                )
                for k in range(1, n_rows)
            ]

        def start(self):
            for copy in self.copies:
                copy.start()

        def wait_recv(self):
            for copy in self.copies:
                copy.wait_recv()

        def wait_send(self):
            for copy in self.copies:
                copy.wait_send()

    class Frames:
        def __init__(self, slots, half):
            self.copies = [
                pltpu.make_async_remote_copy(
                    src_ref=slots.at[pl.ds(0, 1)],
                    dst_ref=slots.at[pl.ds(1 + i, 1)],
                    send_sem=tm_send.at[half, i],
                    recv_sem=tm_recv.at[half, i],
                    device_id=device(d, 0),
                    device_id_type=MESH,
                )
                for i, d in enumerate(offsets)
            ]

        def start(self):
            for copy, d in zip(self.copies, offsets):
                pl.when(exists(d))(copy.start)

        def wait_recv(self):
            for copy, d in zip(self.copies, offsets):
                pl.when(exists(-d))(copy.wait_recv)

        def wait_send(self):
            for copy, d in zip(self.copies, offsets):
                pl.when(exists(d))(copy.wait_send)

    members = width // GROUPS
    per_block = float(height * cols * members)
    per_frame = per_block * n_rows
    quarter = lax.rem(lax.broadcasted_iota(jnp.int32, (1, width), 1), 2 * count)

    def local_stats(block):
        packed = jnp.zeros((1, width), jnp.float32)
        for f in range(count):
            values = block[count + f, 1 : height + 1].reshape(height * cols, width).astype(jnp.float32)
            total = jnp.sum(values, axis=0, keepdims=True)
            mean = total * (members / per_block)
            off = values - mean
            squares = jnp.sum(off * off, axis=0, keepdims=True)
            total = group_total(total, members)
            off = mean - total * (1.0 / per_block)
            squares = group_total(squares + off * off * (per_block / members), members)
            packed = jnp.where(quarter == f, total, packed)
            packed = jnp.where(quarter == count + f, squares, packed)
        return packed

    def merged_rows(slots):
        parts = slots[...]
        total = jnp.sum(parts, axis=0, keepdims=True)
        off = parts * (1.0 / per_block) - total * (1.0 / per_frame)
        between = jnp.sum(off * off, axis=0, keepdims=True) * per_block
        return total + jnp.where(quarter < count, 0.0, pltpu.roll(between, count, 1))

    def merged_frames(slots, inside, length):
        parts = slots[...]
        total = jnp.sum(jnp.where(inside, parts, 0.0), axis=0, keepdims=True)
        entries = length.astype(jnp.float32) * per_frame
        mean = group_total(jnp.where(quarter < count, total, 0.0), members) / entries
        off = parts * (1.0 / per_frame) - mean
        between = jnp.sum(jnp.where(inside, off * off, 0.0), axis=0, keepdims=True) * per_frame
        var = group_total(jnp.where(quarter < count, between, total), members) / entries
        return mean, lax.rsqrt(var + 1e-6)

    def activate(block, stats, gain, shift):
        top = row == 0
        bottom = row == n_rows - 1
        for f in range(2 * count):
            mean, scale = stats[max(f - count, 0)]
            factor = scale * gain
            for i in range(height + 2):
                v = (block[f, i].astype(jnp.float32) - mean) * factor + shift
                v = v * (0.5 * jnp.tanh(0.5 * v) + 0.5)
                if i == 0:
                    v = jnp.where(top, 0.0, v)
                if i == height + 1:
                    v = jnp.where(bottom, 0.0, v)
                act[f, i] = v.astype(jnp.bfloat16)

    def conv(taps, sources):
        lefts = []
        for f in range(count):
            pieces = []
            for dt in range(3):
                for dy in range(3):
                    pieces.append(
                        act[sources[f][dt], dy : dy + height].reshape(height * cols, width)
                    )
            lefts.append(jnp.concatenate(pieces, axis=1))
        left = jnp.concatenate(lefts, axis=0)
        right = taps[...].reshape(9 * width, 3 * width)
        return jnp.dot(left, right, preferred_element_type=jnp.float32)

    column = lax.broadcasted_iota(jnp.int32, (cols, width), 0)

    def joined(wide, i):
        y = wide[i * cols : (i + 1) * cols]
        before = pltpu.roll(y[:, :width], 1, 0)
        after = pltpu.roll(y[:, 2 * width :], cols - 1, 0)
        return (
            y[:, width : 2 * width]
            + jnp.where(column == 0, 0.0, before)
            + jnp.where(column == cols - 1, 0.0, after)
        )

    load_frames.wait()
    rows_one[pl.ds(0, 1)] = local_stats(raw)
    pl.semaphore_wait(barrier, expected)
    row_sums = Rows(rows_one, 0)
    row_sums.start()
    halo_one = Halo(raw, 0)
    halo_one.start()

    load_lens.wait()
    starts, stops = [], []
    for f in range(count):
        start = jnp.int32(0)
        stop = jnp.int32(0)
        offset = jnp.int32(0)
        for v in range(videos):
            size = lens[v]
            here = offset <= first + f
            start = jnp.where(here, offset, start)
            stop = jnp.where(here, offset + size, stop)
            offset = offset + size
        starts.append(start)
        stops.append(stop)
    slot = lax.broadcasted_iota(jnp.int32, tms_one.shape, 0)
    lane = lax.broadcasted_iota(jnp.int32, tms_one.shape, 1)
    far = (slot + 1) // 2
    home = tm - jnp.where(lax.rem(slot, 2) == 1, far, -far)
    frame = home * count + lax.rem(lane, count)
    known = slot <= len(offsets)
    inside = [known & (frame >= starts[f]) & (frame < stops[f]) for f in range(count)]
    sources = [
        [jnp.maximum(f + dt, starts[f] - first + 2) for dt in range(3)] for f in range(count)
    ]

    row_sums.wait_recv()
    tms_one[pl.ds(0, 1)] = merged_rows(rows_one)
    tm_sums = Frames(tms_one, 0)
    tm_sums.start()
    for load in load_vecs:
        load.wait()
    tm_sums.wait_recv()
    stats = [merged_frames(tms_one, inside[f], stops[f] - starts[f]) for f in range(count)]
    halo_one.wait_recv()
    activate(raw, stats, vecs[0:1], vecs[1:2])
    for load in load_one:
        load.wait()
    wide = conv(taps_one, sources)
    for f in range(count):
        for i in range(height):
            mid[count + f, 1 + i] = (joined(wide, f * height + i) + vecs[2:3]).astype(jnp.bfloat16)
    row_sums.wait_send()
    tm_sums.wait_send()
    halo_one.wait_send()

    rows_two[pl.ds(0, 1)] = local_stats(mid)
    row_sums = Rows(rows_two, 1)
    row_sums.start()
    halo_two = Halo(mid, 1)
    halo_two.start()
    row_sums.wait_recv()
    tms_two[pl.ds(0, 1)] = merged_rows(rows_two)
    tm_sums = Frames(tms_two, 1)
    tm_sums.start()
    tm_sums.wait_recv()
    stats = [merged_frames(tms_two, inside[f], stops[f] - starts[f]) for f in range(count)]
    halo_two.wait_recv()
    activate(mid, stats, vecs[3:4], vecs[4:5])
    for load in load_two:
        load.wait()
    wide = conv(taps_two, sources)
    stores = []
    for f in range(count):
        for i in range(height):
            result[f, i] = (
                joined(wide, f * height + i) + vecs[5:6] + raw[count + f, 1 + i].astype(jnp.float32)
            )
        stores.append(pltpu.make_async_copy(result.at[f], out.at[f], out_sem.at[f]))
        stores[-1].start()
    row_sums.wait_send()
    tm_sums.wait_send()
    halo_two.wait_send()
    for store in stores:
        store.wait()


def per_device(n_tm, n_rows, *args):
    frames, lengths = args[0], args[1]
    count, height, cols, width = frames.shape
    near = len(tm_offsets(n_tm, count))
    window = -(-(1 + near) // 8) * 8
    block = pltpu.VMEM((2 * count, height + 2, cols, width), jnp.bfloat16)
    taps = pltpu.VMEM((3, 3, width, 3 * width), jnp.bfloat16)
    return pl.pallas_call(
        functools.partial(kernel, n_tm, n_rows),
        out_shape=jax.ShapeDtypeStruct(frames.shape, jnp.float32),
        in_specs=[pl.BlockSpec(memory_space=pl.ANY)] * len(args),
        out_specs=pl.BlockSpec(memory_space=pl.ANY),
        scratch_shapes=[
            block, block, block, taps, taps,
            pltpu.VMEM((8, width), jnp.float32),
            pltpu.SMEM(lengths.shape, jnp.int32),
            pltpu.VMEM((n_rows, width), jnp.float32),
            pltpu.VMEM((n_rows, width), jnp.float32),
            pltpu.VMEM((window, width), jnp.float32),
            pltpu.VMEM((window, width), jnp.float32),
            pltpu.VMEM(frames.shape, jnp.float32),
            pltpu.SemaphoreType.DMA((14,)),
            pltpu.SemaphoreType.DMA((2, 5)),
            pltpu.SemaphoreType.DMA((2, 5)),
            pltpu.SemaphoreType.DMA((2, n_rows)),
            pltpu.SemaphoreType.DMA((2, n_rows)),
            pltpu.SemaphoreType.DMA((2, near)),
            pltpu.SemaphoreType.DMA((2, near)),
            pltpu.SemaphoreType.DMA((count,)),
        ],
        compiler_params=pltpu.CompilerParams(
            collective_id=0, has_side_effects=True, vmem_limit_bytes=63 * 1024 * 1024
        ),
        name="residual_block",
    )(*args)


def solution(mesh):
    placed = (P("tm", "rows", None, None), P(), P(), P(), P(), P(), P(), P(), P(), P())
    return jax.shard_map(
        functools.partial(per_device, mesh.shape["tm"], mesh.shape["rows"]),
        mesh=mesh,
        in_specs=placed,
        out_specs=P("tm", "rows", None, None),
        check_vma=False,
    )
```

time: 42.2 us -> 37.9 us (0.90)
  the two profiles are of different devices: /device:TPU:1 before, /device:TPU:64 now
where the time goes in v2:
time: 37.9 us; the launch traced here: 37.7 us
  Pallas kernels  35.9 us (95%)
  local copies, waits for them, and re-layouts  1.77 us (5%)
    pallas_call x1, Pallas kernels, per_device(): pl.pallas_call(functools.partial(kernel, n_tm, n_rows), out_shape=jax.Sha...  35.9 us
    unnamed x1, local copies, waits for them, and re-layouts  1.77 us

profile of v2, /device:TPU:64, one launch (start us, length us, event | category | flops | bytes accessed | tf_op | source)
XLA Modules:
  0.0 37.7 jit_solution(1362840244107176443)
XLA Ops:
  0.0 35.9 %residual_block.1 = f32[2,8,48,128]{3,2,1,0:T(8,128)} custom-call(bf16[2,8,48,128]{3,2,1,0:T(8,128)(2,1)} %frames.1, s32[8]{0:T(128)} %lengths.1, f32[128]{0:T(128)} %gain_one.1, f32[128]{0:T(128)} %shift_one.1, bf16[3,3,3,128,128]{4,3,2,1,0:T(8,128)(2,1)} %conv_one.1, f32[128]{0:T(128)} %bias_one.1, f32[128]{0:T(128)} %gain_two.1, f32[128]{0:T(128)} %shift_two.1, ...), custom_call_target="tpu_custom_call" | custom-call | tf_op jit(solution)/shard_map/residual_block/pallas_call | solution.py:368
  35.9 1.8 %copy.12 = f32[2,8,48,128]{3,2,1,0:T(8,128)} copy(f32[2,8,48,128]{3,2,1,0:T(8,128)} %residual_block.1) | data formatting | bytes 786432

commit v3 on v2

--- a/solution.py
+++ b/solution.py
@@ -37,8 +37,8 @@
     n_tm, n_rows,
     frames, lengths, gain_one, shift_one, conv_one, bias_one, gain_two, shift_two, conv_two, bias_two,
     out,
-    raw, mid, act, taps_one, taps_two, vecs, lens, rows_one, rows_two, tms_one, tms_two, result,
-    load_sem, halo_send, halo_recv, row_send, row_recv, tm_send, tm_recv, out_sem,
+    raw, mid, act, taps_one, taps_two, vecs, lens, rows_one, rows_two, tms_one, tms_two,
+    load_sem, halo_send, halo_recv, row_send, row_recv, tm_send, tm_recv,
 ):
     count, height, cols, width = frames.shape
     videos = lengths.shape[0]
@@ -343,19 +343,14 @@
     for load in load_two:
         load.wait()
     wide = conv(taps_two, sources)
-    stores = []
     for f in range(count):
         for i in range(height):
-            result[f, i] = (
+            out[f, i] = (
                 joined(wide, f * height + i) + vecs[5:6] + raw[count + f, 1 + i].astype(jnp.float32)
             )
-        stores.append(pltpu.make_async_copy(result.at[f], out.at[f], out_sem.at[f]))
-        stores[-1].start()
     row_sums.wait_send()
     tm_sums.wait_send()
     halo_two.wait_send()
-    for store in stores:
-        store.wait()
 
 
 def per_device(n_tm, n_rows, *args):
@@ -367,9 +362,9 @@
     taps = pltpu.VMEM((3, 3, width, 3 * width), jnp.bfloat16)
     return pl.pallas_call(
         functools.partial(kernel, n_tm, n_rows),
-        out_shape=jax.ShapeDtypeStruct(frames.shape, jnp.float32),
+        out_shape=pltpu.VMEM(frames.shape, jnp.float32),
         in_specs=[pl.BlockSpec(memory_space=pl.ANY)] * len(args),
-        out_specs=pl.BlockSpec(memory_space=pl.ANY),
+        out_specs=pl.BlockSpec(memory_space=pltpu.VMEM),
         scratch_shapes=[
             block, block, block, taps, taps,
             pltpu.VMEM((8, width), jnp.float32),
@@ -378,7 +373,6 @@
             pltpu.VMEM((n_rows, width), jnp.float32),
             pltpu.VMEM((window, width), jnp.float32),
             pltpu.VMEM((window, width), jnp.float32),
-            pltpu.VMEM(frames.shape, jnp.float32),
             pltpu.SemaphoreType.DMA((14,)),
             pltpu.SemaphoreType.DMA((2, 5)),
             pltpu.SemaphoreType.DMA((2, 5)),
@@ -386,13 +380,12 @@
             pltpu.SemaphoreType.DMA((2, n_rows)),
             pltpu.SemaphoreType.DMA((2, near)),
             pltpu.SemaphoreType.DMA((2, near)),
-            pltpu.SemaphoreType.DMA((count,)),
         ],
         compiler_params=pltpu.CompilerParams(
-            collective_id=0, has_side_effects=True, vmem_limit_bytes=63 * 1024 * 1024
+            collective_id=0, has_side_effects=True, vmem_limit_bytes=40 * 1024 * 1024
         ),
         name="residual_block",
-    )(*args)
+    )(*[pltpu.with_memory_space_constraint(a, pltpu.HBM) for a in args])
 
 
 def solution(mesh):

time: 37.9 us -> 36.2 us (0.955)
  local copies, waits for them, and re-layouts: 1.77 us -> 0.75 us
  Pallas kernels: 35.9 us -> 35.3 us
    unnamed x1, local copies, waits for them, and re-layouts: 1.77 us -> 0.75 us
    pallas_call x1, Pallas kernels: 35.9 us -> 35.3 us  [per_device(): pl.pallas_call(functools.partial(kernel, n_tm, n_rows), out_shape=pltpu.V...]
where the time goes in v3:
time: 36.2 us; the launch traced here: 36 us
  Pallas kernels  35.3 us (98%)
  local copies, waits for them, and re-layouts  0.75 us (2%)
    pallas_call x1, Pallas kernels, per_device(): pl.pallas_call(functools.partial(kernel, n_tm, n_rows), out_shape=pltpu.V...  35.3 us
    unnamed x1, local copies, waits for them, and re-layouts  0.75 us

profile of v3, /device:TPU:64, one launch (start us, length us, event | category | flops | bytes accessed | tf_op | source)
XLA Modules:
  0.0 36.0 jit_solution(13220327978834835558)
XLA Ops:
  0.0 35.3 %residual_block.1 = f32[2,8,48,128]{3,2,1,0:T(8,128)S(1)} custom-call(bf16[2,8,48,128]{3,2,1,0:T(8,128)(2,1)} %frames.1, s32[8]{0:T(128)} %lengths.1, f32[128]{0:T(128)} %gain_one.1, f32[128]{0:T(128)} %shift_one.1, bf16[3,3,3,128,128]{4,3,2,1,0:T(8,128)(2,1)} %conv_one.1, f32[128]{0:T(128)} %bias_one.1, f32[128]{0:T(128)} %gain_two.1, f32[128]{0:T(128)} %shift_two.1, ...), custom_call_target="tpu_custom_call" | custom-call | tf_op jit(solution)/shard_map/residual_block/pallas_call | solution.py:363
  35.3 0.7 %copy.12 = f32[2,8,48,128]{3,2,1,0:T(8,128)} copy(f32[2,8,48,128]{3,2,1,0:T(8,128)S(1)} %residual_block.1) | data formatting | bytes 786432

commit v4 on v3

v4 whole, which is shorter than its diff:
```python
import functools

import jax
import jax.numpy as jnp
from jax import lax
from jax.experimental import pallas as pl
from jax.experimental.pallas import tpu as pltpu
from jax.sharding import PartitionSpec as P

GROUPS = 32
MOST = 16
MESH = pl.DeviceIdType.MESH


def tm_offsets(n_tm, count):
    reach = min(-(-(MOST - 1) // count), n_tm - 1)
    return [d for far in range(1, reach + 1) for d in (far, -far)]


def tm_hops(d):
    return abs(d) // 4 + min(abs(d) % 4, 4 - abs(d) % 4)


def wrapped(index, offset, size):
    return lax.rem(index + (offset + size), size)


def neighbours(row):
    lanes = row.shape[1]
    return {s: pltpu.roll(row, s % lanes, 1) if s else row for s in range(-3, 4)}


def by_place(place, choices):
    picked = choices[-1]
    for i in range(len(choices) - 1):
        picked = jnp.where(place == i, choices[i], picked)
    return picked


def group_total(row, place):
    near = neighbours(row)
    sums = [near[i] + near[i - 1] + (near[i - 2] + near[i - 3]) for i in range(4)]
    return by_place(place, sums)


def await_signals(semaphore, number):
    @pl.when(number > 0)
    def _():
        pl.semaphore_wait(semaphore, number)


def kernel(
    n_tm, n_rows,
    frames, lengths, gain_one, shift_one, conv_one, bias_one, gain_two, shift_two, conv_two, bias_two,
    out,
    raw, mid, act, taps_one, taps_two, vecs, lens, rows_one, rows_two, tms_one, tms_two,
    ready, load_sem, halo_send, halo_recv, row_send, row_recv, tm_send, tm_recv,
):
    count, height, cols, width = frames.shape
    videos = lengths.shape[0]
    tm = lax.axis_index("tm")
    row = lax.axis_index("rows")
    first = tm * count
    offsets = tm_offsets(n_tm, count)

    load_frames = pltpu.make_async_copy(
        frames, raw.at[pl.ds(count, count), pl.ds(1, height)], load_sem.at[0]
    )
    load_frames.start()

    def exists(d):
        return (tm + d >= 0) & (tm + d < n_tm)

    def device(d, k):
        return {"tm": tm + d, "rows": wrapped(row, k, n_rows)}

    host = n_rows > 1 and 1
    hosting = row == host
    reach = max(offsets)
    below = jnp.minimum(tm, reach)
    above = jnp.minimum(n_tm - 1 - tm, reach)
    barrier = pltpu.get_barrier_semaphore()
    full, answers, complete = ready.at[0], ready.at[1], ready.at[2]

    def signal(semaphore, target):
        pl.semaphore_signal(semaphore, inc=1, device_id=target, device_id_type=MESH)

    def tell_rows(semaphore):
        @pl.when(hosting)
        def _():
            for k in sorted(range(1, n_rows), key=lambda k: -min(k, n_rows - k)):
                signal(semaphore, device(0, k))

    tell_rows(barrier)
    for d in range(reach, 0, -1):

        @pl.when(exists(d))
        def _(d=d):
            signal(barrier, device(d, 0))

    announced = below + jnp.where(hosting, 0, 1)

    def answer():
        for d in range(1, reach + 1):

            @pl.when(exists(-d))
            def _(d=d):
                signal(ready.at[2 + d], device(-d, 0))

        @pl.when(jnp.logical_not(hosting))
        def _():
            signal(answers, {"tm": tm, "rows": host})

    load_lens = pltpu.make_async_copy(lengths, lens, load_sem.at[1])
    load_lens.start()
    for i, vec in enumerate((gain_one, shift_one, bias_one, gain_two, shift_two, bias_two)):
        pltpu.make_async_copy(vec, vecs.at[i], load_sem.at[2]).start()
    for dx in range(3):
        for i, (source, held) in enumerate(((conv_one, taps_one), (conv_two, taps_two))):
            pltpu.make_async_copy(
                source.at[:, :, dx], held.at[:, :, :, pl.ds(dx * width, width)], load_sem.at[3 + i]
            ).start()
    load_vecs = pltpu.make_async_copy(vecs.at[pl.ds(0, 6)], vecs.at[pl.ds(0, 6)], load_sem.at[2])
    load_one = pltpu.make_async_copy(taps_one, taps_one, load_sem.at[3])
    load_two = pltpu.make_async_copy(taps_two, taps_two, load_sem.at[4])

    def remote(src, dst, send, recv, d, k):
        return pltpu.make_async_remote_copy(
            src_ref=src,
            dst_ref=dst,
            send_sem=send,
            recv_sem=recv,
            device_id=device(d, k),
            device_id_type=MESH,
        )

    class Halo:
        def __init__(self, block, half):
            own, prior = pl.ds(count, count), pl.ds(0, count)
            whole, last, head = pl.ds(1, height), pl.ds(height, 1), pl.ds(1, 1)
            above, below = pl.ds(0, 1), pl.ds(height + 1, 1)

            def copy(f, src, g, dst, d, k):
                sems = halo_send.at[half, d], halo_recv.at[half, d]
                return remote(block.at[f, src], block.at[g, dst], *sems, d, k)

            self.beside = [copy(own, last, own, above, 0, 1), copy(own, head, own, below, 0, -1)]
            self.onward = copy(own, whole, prior, whole, 1, 0)
            self.corners = [copy(own, last, prior, above, 1, 1), copy(own, head, prior, below, 1, -1)]
            edge = block.at[:, pl.ds(0, 1)]
            self.all_beside = remote(edge, edge, halo_send.at[half, 0], halo_recv.at[half, 0], 0, 1)
            front = block.at[prior]
            self.all_onward = remote(front, front, halo_send.at[half, 1], halo_recv.at[half, 1], 0, 1)

        def start_beside(self):
            for copy in self.beside:
                copy.start()

        def start_onward(self):
            pl.when(exists(1))(self.onward.start)

        def start_corners(self):
            @pl.when(exists(1))
            def _():
                for copy in self.corners:
                    copy.start()

        def wait_recv(self):
            self.all_beside.wait_recv()
            pl.when(exists(-1))(self.all_onward.wait_recv)

        def wait_send(self):
            self.all_beside.wait_send()
            pl.when(exists(1))(self.all_onward.wait_send)

    class Rows:
        def __init__(self, slots, half):
            sems = row_send.at[half], row_recv.at[half]
            self.copies = [
                remote(slots.at[pl.ds(0, 1)], slots.at[pl.ds(k, 1)], *sems, 0, k) for k in range(1, n_rows)
            ]
            others = slots.at[pl.ds(1, n_rows - 1)]
            self.all = remote(others, others, *sems, 0, 1)

        def start(self):
            for k in sorted(range(1, n_rows), key=lambda k: -min(k, n_rows - k)):
                self.copies[k - 1].start()

    class Frames:
        def __init__(self, slots, half):
            sems = tm_send.at[half], tm_recv.at[half]
            self.copies = {
                d: remote(slots.at[pl.ds(0, 1)], slots.at[pl.ds(1 + i, 1)], *sems, d, 0)
                for i, d in enumerate(offsets)
            }
            self.all = {}
            for n in range(reach, 2 * reach + 1):
                others = slots.at[pl.ds(1, n)]
                self.all[n] = remote(others, others, *sems, 0, 1)

        def start(self, *signs):
            for d in sorted(range(1, reach + 1), key=lambda d: -tm_hops(d)):
                for sign in signs:
                    pl.when(exists(sign * d))(self.copies[sign * d].start)

        def wait_recv(self):
            for n in self.all:
                pl.when(below + above == n)(self.all[n].wait_recv)

        def wait_send(self):
            for n in self.all:
                pl.when(below + above == n)(self.all[n].wait_send)

    members = width // GROUPS
    per_block = float(height * cols * members)
    place = lax.rem(lax.broadcasted_iota(jnp.int32, (1, width), 1), members)
    odd = lax.rem(place, 2) == 1
    head = place < 2

    def local_stats(block):
        totals, squares = [], []
        for f in range(count):
            values = block[count + f, 1 : height + 1].reshape(height * cols, width).astype(jnp.float32)
            total = jnp.sum(values, axis=0, keepdims=True)
            mean = total * (members / per_block)
            off = values - mean
            square = jnp.sum(off * off, axis=0, keepdims=True)
            total = group_total(total, place)
            off = mean - total * (1.0 / per_block)
            totals.append(total)
            squares.append(group_total(square + off * off * (per_block / members), place))
        return by_place(place, totals + squares)

    def video_sums(slots, inside, entries):
        parts = slots[...]
        merged = []
        for f in range(count):
            total = jnp.sum(jnp.where(inside[f], parts, 0.0), axis=0, keepdims=True)
            total = total + jnp.where(odd, pltpu.roll(total, 1, 1), pltpu.roll(total, width - 1, 1))
            off = parts * (1.0 / per_block) - total * (1.0 / entries[f])
            between = jnp.sum(jnp.where(inside[f], off * off, 0.0), axis=0, keepdims=True) * per_block
            between = pltpu.roll(between, 2, 1) + jnp.where(
                odd, pltpu.roll(between, 3, 1), pltpu.roll(between, 1, 1)
            )
            merged.append(total + jnp.where(head, 0.0, between))
        return jnp.where(odd, merged[1], merged[0])

    def video_stats(slots, entries):
        parts = slots[...]
        share = jnp.where(odd, entries[1], entries[0])
        total = jnp.sum(parts, axis=0, keepdims=True)
        mean = total / (share * n_rows)
        off = parts * (1.0 / share) - mean
        between = jnp.sum(off * off, axis=0, keepdims=True) * share
        var = (total + pltpu.roll(between, 2, 1)) / (share * n_rows)
        near = neighbours(jnp.where(head, mean, lax.rsqrt(var + 1e-6)))
        spread = [by_place(place, [near[i - k] for i in range(4)]) for k in range(4)]
        return [(spread[f], spread[count + f]) for f in range(count)]

    def activate(block, stats, gain, shift):
        top = row == 0
        bottom = row == n_rows - 1
        for f in range(2 * count):
            mean, scale = stats[max(f - count, 0)]
            factor = scale * gain
            for i in range(height + 2):
                v = (block[f, i].astype(jnp.float32) - mean) * factor + shift
                v = v * (0.5 * jnp.tanh(0.5 * v) + 0.5)
                if i == 0:
                    v = jnp.where(top, 0.0, v)
                if i == height + 1:
                    v = jnp.where(bottom, 0.0, v)
                act[f, i] = v.astype(jnp.bfloat16)

    def conv(taps, sources):
        lefts = []
        for f in range(count):
            pieces = []
            for dt in range(3):
                for dy in range(3):
                    pieces.append(
                        act[sources[f][dt], dy : dy + height].reshape(height * cols, width)
                    )
            lefts.append(jnp.concatenate(pieces, axis=1))
        left = jnp.concatenate(lefts, axis=0)
        right = taps[...].reshape(9 * width, 3 * width)
        return jnp.dot(left, right, preferred_element_type=jnp.float32)

    column = lax.broadcasted_iota(jnp.int32, (cols, width), 0)

    def joined(wide, i):
        y = wide[i * cols : (i + 1) * cols]
        before = pltpu.roll(y[:, :width], 1, 0)
        after = pltpu.roll(y[:, 2 * width :], cols - 1, 0)
        return (
            y[:, width : 2 * width]
            + jnp.where(column == 0, 0.0, before)
            + jnp.where(column == cols - 1, 0.0, after)
        )

    load_frames.wait()
    tms_one[pl.ds(0, 1)] = local_stats(raw)
    await_signals(barrier, announced)
    tm_sums = Frames(tms_one, 0)
    tm_sums.start(-1)
    answer()

    load_lens.wait()
    starts, stops = [], []
    for f in range(count):
        start = jnp.int32(0)
        stop = jnp.int32(0)
        offset = jnp.int32(0)
        for v in range(videos):
            size = lens[v]
            here = offset <= first + f
            start = jnp.where(here, offset, start)
            stop = jnp.where(here, offset + size, stop)
            offset = offset + size
        starts.append(start)
        stops.append(stop)
    entries = [(stops[f] - starts[f]).astype(jnp.float32) * per_block for f in range(count)]
    slot = lax.broadcasted_iota(jnp.int32, tms_one.shape, 0)
    lane = lax.broadcasted_iota(jnp.int32, tms_one.shape, 1)
    far = (slot + 1) // 2
    home = tm - jnp.where(lax.rem(slot, 2) == 1, far, -far)
    frame = home * count + lax.rem(lane, count)
    known = slot <= len(offsets)
    inside = [known & (frame >= starts[f]) & (frame < stops[f]) for f in range(count)]
    sources = [
        [jnp.maximum(f + dt, starts[f] - first + 2) for dt in range(3)] for f in range(count)
    ]

    for d in range(1, reach + 1):

        @pl.when(exists(d))
        def _(d=d):
            pl.semaphore_wait(ready.at[2 + d], 1)
            tm_sums.copies[d].start()

    halo_one = Halo(raw, 0)
    halo_one.start_onward()

    @pl.when(hosting)
    def _():
        pl.semaphore_wait(answers, n_rows - 1)

    tell_rows(complete)

    @pl.when(jnp.logical_not(hosting))
    def _():
        pl.semaphore_wait(complete, 1)

    @pl.when(exists(-1))
    def _():
        signal(full, device(-1, 0))

    tm_sums.wait_recv()
    rows_one[pl.ds(0, 1)] = video_sums(tms_one, inside, entries)
    row_sums = Rows(rows_one, 0)
    row_sums.start()
    halo_one.start_beside()

    @pl.when(exists(1))
    def _():
        pl.semaphore_wait(full, 1)

    halo_one.start_corners()
    load_vecs.wait()
    row_sums.all.wait_recv()
    stats = video_stats(rows_one, entries)
    halo_one.wait_recv()
    activate(raw, stats, vecs[0:1], vecs[1:2])
    load_one.wait()
    wide = conv(taps_one, sources)
    for f in range(count):
        for i in range(height):
            mid[count + f, 1 + i] = (joined(wide, f * height + i) + vecs[2:3]).astype(jnp.bfloat16)
    tm_sums.wait_send()
    row_sums.all.wait_send()
    halo_one.wait_send()

    tms_two[pl.ds(0, 1)] = local_stats(mid)
    tm_sums = Frames(tms_two, 1)
    tm_sums.start(-1, 1)
    halo_two = Halo(mid, 1)
    halo_two.start_beside()
    halo_two.start_corners()
    halo_two.start_onward()
    tm_sums.wait_recv()
    rows_two[pl.ds(0, 1)] = video_sums(tms_two, inside, entries)
    row_sums = Rows(rows_two, 1)
    row_sums.start()
    row_sums.all.wait_recv()
    stats = video_stats(rows_two, entries)
    halo_two.wait_recv()
    activate(mid, stats, vecs[3:4], vecs[4:5])
    load_two.wait()
    wide = conv(taps_two, sources)
    for f in range(count):
        for i in range(height):
            out[f, i] = (
                joined(wide, f * height + i) + vecs[5:6] + raw[count + f, 1 + i].astype(jnp.float32)
            )
    tm_sums.wait_send()
    row_sums.all.wait_send()
    halo_two.wait_send()


def per_device(n_tm, n_rows, *args):
    frames, lengths = args[0], args[1]
    count, height, cols, width = frames.shape
    near = len(tm_offsets(n_tm, count))
    window = -(-(1 + near) // 8) * 8
    block = pltpu.VMEM((2 * count, height + 2, cols, width), jnp.bfloat16)
    taps = pltpu.VMEM((3, 3, width, 3 * width), jnp.bfloat16)
    return pl.pallas_call(
        functools.partial(kernel, n_tm, n_rows),
        out_shape=pltpu.VMEM(frames.shape, jnp.float32),
        in_specs=[pl.BlockSpec(memory_space=pl.ANY)] * len(args),
        out_specs=pl.BlockSpec(memory_space=pltpu.VMEM),
        scratch_shapes=[
            block, block, block, taps, taps,
            pltpu.VMEM((8, width), jnp.float32),
            pltpu.SMEM(lengths.shape, jnp.int32),
            pltpu.VMEM((n_rows, width), jnp.float32),
            pltpu.VMEM((n_rows, width), jnp.float32),
            pltpu.VMEM((window, width), jnp.float32),
            pltpu.VMEM((window, width), jnp.float32),
            pltpu.SemaphoreType.REGULAR((3 + near // 2 + 1,)),
            pltpu.SemaphoreType.DMA((5,)),
            pltpu.SemaphoreType.DMA((2, 2)),
            pltpu.SemaphoreType.DMA((2, 2)),
            pltpu.SemaphoreType.DMA((2,)),
            pltpu.SemaphoreType.DMA((2,)),
            pltpu.SemaphoreType.DMA((2,)),
            pltpu.SemaphoreType.DMA((2,)),
        ],
        compiler_params=pltpu.CompilerParams(
            collective_id=0, has_side_effects=True, vmem_limit_bytes=40 * 1024 * 1024
        ),
        name="residual_block",
    )(*[pltpu.with_memory_space_constraint(a, pltpu.HBM) for a in args])


def solution(mesh):
    placed = (P("tm", "rows", None, None), P(), P(), P(), P(), P(), P(), P(), P(), P())
    return jax.shard_map(
        functools.partial(per_device, mesh.shape["tm"], mesh.shape["rows"]),
        mesh=mesh,
        in_specs=placed,
        out_specs=P("tm", "rows", None, None),
        check_vma=False,
    )
```

time: 36.2 us -> 34.2 us (0.945)
  the two profiles are of different devices: /device:TPU:64 before, /device:TPU:128 now
where the time goes in v4:
time: 34.2 us; the launch traced here: 34.1 us
  Pallas kernels  33.3 us (97%)
  local copies, waits for them, and re-layouts  0.75 us (2%)
    pallas_call x1, Pallas kernels, per_device(): pl.pallas_call(functools.partial(kernel, n_tm, n_rows), out_shape=pltpu.V...  33.3 us
    unnamed x1, local copies, waits for them, and re-layouts  0.75 us

profile of v4, /device:TPU:128, one launch (start us, length us, event | category | flops | bytes accessed | tf_op | source)
XLA Modules:
  0.0 34.1 jit_solution(12514975803829879009)
XLA Ops:
  0.0 33.3 %residual_block.1 = f32[2,8,48,128]{3,2,1,0:T(8,128)S(1)} custom-call(bf16[2,8,48,128]{3,2,1,0:T(8,128)(2,1)} %frames.1, s32[8]{0:T(128)} %lengths.1, f32[128]{0:T(128)} %gain_one.1, f32[128]{0:T(128)} %shift_one.1, bf16[3,3,3,128,128]{4,3,2,1,0:T(8,128)(2,1)} %conv_one.1, f32[128]{0:T(128)} %bias_one.1, f32[128]{0:T(128)} %gain_two.1, f32[128]{0:T(128)} %shift_two.1, ...), custom_call_target="tpu_custom_call" | custom-call | tf_op jit(solution)/shard_map/residual_block/pallas_call | solution.py:417
  33.4 0.7 %copy.12 = f32[2,8,48,128]{3,2,1,0:T(8,128)} copy(f32[2,8,48,128]{3,2,1,0:T(8,128)S(1)} %residual_block.1) | data formatting | bytes 786432

commit v5 on v4

--- a/solution.py
+++ b/solution.py
@@ -53,7 +53,7 @@
     n_tm, n_rows,
     frames, lengths, gain_one, shift_one, conv_one, bias_one, gain_two, shift_two, conv_two, bias_two,
     out,
-    raw, mid, act, taps_one, taps_two, vecs, lens, rows_one, rows_two, tms_one, tms_two,
+    raw, mid, taps_one, taps_two, vecs, lens, rows_one, rows_two, tms_one, tms_two,
     ready, load_sem, halo_send, halo_recv, row_send, row_recv, tm_send, tm_recv,
 ):
     count, height, cols, width = frames.shape
@@ -91,13 +91,13 @@
             for k in sorted(range(1, n_rows), key=lambda k: -min(k, n_rows - k)):
                 signal(semaphore, device(0, k))
 
-    tell_rows(barrier)
-    for d in range(reach, 0, -1):
+    for d in range(1, reach + 1):
 
         @pl.when(exists(d))
         def _(d=d):
             signal(barrier, device(d, 0))
 
+    tell_rows(barrier)
     announced = below + jnp.where(hosting, 0, 1)
 
     def answer():
@@ -145,7 +145,8 @@
                 return remote(block.at[f, src], block.at[g, dst], *sems, d, k)
 
             self.beside = [copy(own, last, own, above, 0, 1), copy(own, head, own, below, 0, -1)]
-            self.onward = copy(own, whole, prior, whole, 1, 0)
+            halves = [(pl.ds(count + f, 1), pl.ds(f, 1)) for f in range(count)]
+            self.onward = [copy(src, whole, dst, whole, 1, 0) for src, dst in halves]
             self.corners = [copy(own, last, prior, above, 1, 1), copy(own, head, prior, below, 1, -1)]
             edge = block.at[:, pl.ds(0, 1)]
             self.all_beside = remote(edge, edge, halo_send.at[half, 0], halo_recv.at[half, 0], 0, 1)
@@ -156,8 +157,11 @@
             for copy in self.beside:
                 copy.start()
 
-        def start_onward(self):
-            pl.when(exists(1))(self.onward.start)
+        def start_onward(self, *halves):
+            @pl.when(exists(1))
+            def _():
+                for half in halves:
+                    self.onward[half].start()
 
         def start_corners(self):
             @pl.when(exists(1))
@@ -217,18 +221,24 @@
     odd = lax.rem(place, 2) == 1
     head = place < 2
 
-    def local_stats(block):
+    def local_stats(frames_rows):
         totals, squares = [], []
-        for f in range(count):
-            values = block[count + f, 1 : height + 1].reshape(height * cols, width).astype(jnp.float32)
-            total = jnp.sum(values, axis=0, keepdims=True)
-            mean = total * (members / per_block)
-            off = values - mean
-            square = jnp.sum(off * off, axis=0, keepdims=True)
-            total = group_total(total, place)
-            off = mean - total * (1.0 / per_block)
+        for rows in frames_rows:
+            near = jnp.sum(rows[0].astype(jnp.float32), axis=0, keepdims=True) * (1.0 / cols)
+            first_sum = jnp.zeros((cols, width), jnp.float32)
+            second_sum = jnp.zeros((cols, width), jnp.float32)
+            for values in rows:
+                off = values.astype(jnp.float32) - near
+                first_sum = first_sum + off
+                second_sum = second_sum + off * off
+            first_sum = jnp.sum(first_sum, axis=0, keepdims=True)
+            second_sum = jnp.sum(second_sum, axis=0, keepdims=True)
+            shift = first_sum * (1.0 / (height * cols))
+            total = group_total(first_sum + near * float(height * cols), place)
+            off = near + shift - total * (1.0 / per_block)
+            square = second_sum - first_sum * shift + off * off * float(height * cols)
             totals.append(total)
-            squares.append(group_total(square + off * off * (per_block / members), place))
+            squares.append(group_total(square, place))
         return by_place(place, totals + squares)
 
     def video_sums(slots, inside, entries):
@@ -257,49 +267,73 @@
         spread = [by_place(place, [near[i - k] for i in range(4)]) for k in range(4)]
         return [(spread[f], spread[count + f]) for f in range(count)]
 
-    def activate(block, stats, gain, shift):
-        top = row == 0
-        bottom = row == n_rows - 1
-        for f in range(2 * count):
+    column = lax.broadcasted_iota(jnp.int32, (cols, width), 0)
+
+    def convolved(block, stats, gain, shift, taps):
+        def active(f, i):
             mean, scale = stats[max(f - count, 0)]
-            factor = scale * gain
-            for i in range(height + 2):
-                v = (block[f, i].astype(jnp.float32) - mean) * factor + shift
-                v = v * (0.5 * jnp.tanh(0.5 * v) + 0.5)
-                if i == 0:
-                    v = jnp.where(top, 0.0, v)
-                if i == height + 1:
-                    v = jnp.where(bottom, 0.0, v)
-                act[f, i] = v.astype(jnp.bfloat16)
-
-    def conv(taps, sources):
-        lefts = []
+            v = (block[f, i].astype(jnp.float32) - mean) * (scale * gain) + shift
+            v = v * (0.5 * jnp.tanh(0.5 * v) + 0.5)
+            if i == 0:
+                v = jnp.where(row == 0, 0.0, v)
+            if i == height + 1:
+                v = jnp.where(row == n_rows - 1, 0.0, v)
+            return v.astype(jnp.bfloat16)
+
+        seen = [[[], [], []] for _ in range(count)]
+        for i in range(height + 2):
+            a, b, c, d = [active(f, i) for f in range(2 * count)]
+            b = jnp.where(starts[0] < first, b, c)
+            seen[0][0].append(jnp.where(starts[0] < first - 1, a, b))
+            seen[0][1].append(b)
+            seen[0][2].append(c)
+            seen[1][0].append(jnp.where(starts[1] > first, d, b))
+            seen[1][1].append(jnp.where(starts[1] > first, d, c))
+            seen[1][2].append(d)
+        right = taps[...].reshape(9 * width, 3 * width)
+        results = []
         for f in range(count):
-            pieces = []
-            for dt in range(3):
-                for dy in range(3):
-                    pieces.append(
-                        act[sources[f][dt], dy : dy + height].reshape(height * cols, width)
-                    )
-            lefts.append(jnp.concatenate(pieces, axis=1))
-        left = jnp.concatenate(lefts, axis=0)
-        right = taps[...].reshape(9 * width, 3 * width)
-        return jnp.dot(left, right, preferred_element_type=jnp.float32)
-
-    column = lax.broadcasted_iota(jnp.int32, (cols, width), 0)
-
-    def joined(wide, i):
-        y = wide[i * cols : (i + 1) * cols]
-        before = pltpu.roll(y[:, :width], 1, 0)
-        after = pltpu.roll(y[:, 2 * width :], cols - 1, 0)
-        return (
-            y[:, width : 2 * width]
-            + jnp.where(column == 0, 0.0, before)
-            + jnp.where(column == cols - 1, 0.0, after)
-        )
+            pieces = [
+                jnp.concatenate(seen[f][dt][dy : dy + height], axis=0) for dt in range(3) for dy in range(3)
+            ]
+            wide = jnp.dot(jnp.concatenate(pieces, axis=1), right, preferred_element_type=jnp.float32)
+            rows = []
+            for i in range(height):
+                y = wide[i * cols : (i + 1) * cols]
+                before = pltpu.roll(y[:, :width], 1, 0)
+                after = pltpu.roll(y[:, 2 * width :], cols - 1, 0)
+                rows.append(
+                    y[:, width : 2 * width]
+                    + jnp.where(column == 0, 0.0, before)
+                    + jnp.where(column == cols - 1, 0.0, after)
+                )
+            results.append(rows)
+        return results
+
+    def frame_sums(slots):
+        parts = slots[...]
+        total = jnp.sum(parts, axis=0, keepdims=True)
+        off = parts * (1.0 / per_block) - total * (1.0 / (per_block * n_rows))
+        between = jnp.sum(off * off, axis=0, keepdims=True) * per_block
+        return total + jnp.where(head, 0.0, pltpu.roll(between, 2, 1))
+
+    def frame_stats(slots, inside, entries):
+        parts = slots[...]
+        per_frame = per_block * n_rows
+        stats = []
+        for f in range(count):
+            total = jnp.sum(jnp.where(inside[f], parts, 0.0), axis=0, keepdims=True)
+            mean = group_total(jnp.where(head, total, 0.0), place) / (entries[f] * n_rows)
+            off = parts * (1.0 / per_frame) - mean
+            between = jnp.sum(jnp.where(inside[f], off * off, 0.0), axis=0, keepdims=True) * per_frame
+            var = group_total(jnp.where(head, between, total), place) / (entries[f] * n_rows)
+            stats.append((mean, lax.rsqrt(var + 1e-6)))
+        return stats
 
     load_frames.wait()
-    tms_one[pl.ds(0, 1)] = local_stats(raw)
+    tms_one[pl.ds(0, 1)] = local_stats(
+        [[raw[count + f, 1 + i] for i in range(height)] for f in range(count)]
+    )
     await_signals(barrier, announced)
     tm_sums = Frames(tms_one, 0)
     tm_sums.start(-1)
@@ -327,10 +361,8 @@
     frame = home * count + lax.rem(lane, count)
     known = slot <= len(offsets)
     inside = [known & (frame >= starts[f]) & (frame < stops[f]) for f in range(count)]
-    sources = [
-        [jnp.maximum(f + dt, starts[f] - first + 2) for dt in range(3)] for f in range(count)
-    ]
-
+
+    halo_one = Halo(raw, 0)
     for d in range(1, reach + 1):
 
         @pl.when(exists(d))
@@ -338,8 +370,10 @@
             pl.semaphore_wait(ready.at[2 + d], 1)
             tm_sums.copies[d].start()
 
-    halo_one = Halo(raw, 0)
-    halo_one.start_onward()
+        if d == reach // 2:
+            halo_one.start_onward(0)
+
+    halo_one.start_onward(1)
 
     @pl.when(hosting)
     def _():
@@ -370,40 +404,37 @@
     row_sums.all.wait_recv()
     stats = video_stats(rows_one, entries)
     halo_one.wait_recv()
-    activate(raw, stats, vecs[0:1], vecs[1:2])
     load_one.wait()
-    wide = conv(taps_one, sources)
+    results = convolved(raw, stats, vecs[0:1], vecs[1:2], taps_one)
+    results = [[(y + vecs[2:3]).astype(jnp.bfloat16) for y in rows] for rows in results]
     for f in range(count):
         for i in range(height):
-            mid[count + f, 1 + i] = (joined(wide, f * height + i) + vecs[2:3]).astype(jnp.bfloat16)
+            mid[count + f, 1 + i] = results[f][i]
+    rows_two[pl.ds(0, 1)] = local_stats(results)
+    row_sums_two = Rows(rows_two, 1)
+    row_sums_two.start()
+    halo_two = Halo(mid, 1)
+    halo_two.start_beside()
+    halo_two.start_corners()
+    halo_two.start_onward(0, 1)
     tm_sums.wait_send()
     row_sums.all.wait_send()
     halo_one.wait_send()
 
-    tms_two[pl.ds(0, 1)] = local_stats(mid)
-    tm_sums = Frames(tms_two, 1)
-    tm_sums.start(-1, 1)
-    halo_two = Halo(mid, 1)
-    halo_two.start_beside()
-    halo_two.start_corners()
-    halo_two.start_onward()
-    tm_sums.wait_recv()
-    rows_two[pl.ds(0, 1)] = video_sums(tms_two, inside, entries)
-    row_sums = Rows(rows_two, 1)
-    row_sums.start()
-    row_sums.all.wait_recv()
-    stats = video_stats(rows_two, entries)
+    row_sums_two.all.wait_recv()
+    tms_two[pl.ds(0, 1)] = frame_sums(rows_two)
+    tm_sums_two = Frames(tms_two, 1)
+    tm_sums_two.start(-1, 1)
+    tm_sums_two.wait_recv()
+    stats = frame_stats(tms_two, inside, entries)
     halo_two.wait_recv()
-    activate(mid, stats, vecs[3:4], vecs[4:5])
     load_two.wait()
-    wide = conv(taps_two, sources)
+    results = convolved(mid, stats, vecs[3:4], vecs[4:5], taps_two)
     for f in range(count):
         for i in range(height):
-            out[f, i] = (
-                joined(wide, f * height + i) + vecs[5:6] + raw[count + f, 1 + i].astype(jnp.float32)
-            )
-    tm_sums.wait_send()
-    row_sums.all.wait_send()
+            out[f, i] = results[f][i] + vecs[5:6] + raw[count + f, 1 + i].astype(jnp.float32)
+    tm_sums_two.wait_send()
+    row_sums_two.all.wait_send()
     halo_two.wait_send()
 
 
@@ -420,7 +451,7 @@
         in_specs=[pl.BlockSpec(memory_space=pl.ANY)] * len(args),
         out_specs=pl.BlockSpec(memory_space=pltpu.VMEM),
         scratch_shapes=[
-            block, block, block, taps, taps,
+            block, block, taps, taps,
             pltpu.VMEM((8, width), jnp.float32),
             pltpu.SMEM(lengths.shape, jnp.int32),
             pltpu.VMEM((n_rows, width), jnp.float32),

time: 34.2 us -> 33.6 us (0.982)
  Pallas kernels: 33.3 us -> 32.7 us
    pallas_call x1, Pallas kernels: 33.3 us -> 32.7 us  [per_device(): pl.pallas_call(functools.partial(kernel, n_tm, n_rows), out_shape=pltpu.V...]
where the time goes in v5:
time: 33.6 us; the launch traced here: 33.4 us
  Pallas kernels  32.7 us (97%)
  local copies, waits for them, and re-layouts  0.75 us (2%)
    pallas_call x1, Pallas kernels, per_device(): pl.pallas_call(functools.partial(kernel, n_tm, n_rows), out_shape=pltpu.V...  32.7 us
    unnamed x1, local copies, waits for them, and re-layouts  0.75 us

profile of v5, /device:TPU:128, one launch (start us, length us, event | category | flops | bytes accessed | tf_op | source)
XLA Modules:
  0.0 33.4 jit_solution(365474502651030901)
XLA Ops:
  0.0 32.7 %residual_block.1 = f32[2,8,48,128]{3,2,1,0:T(8,128)S(1)} custom-call(bf16[2,8,48,128]{3,2,1,0:T(8,128)(2,1)} %frames.1, s32[8]{0:T(128)} %lengths.1, f32[128]{0:T(128)} %gain_one.1, f32[128]{0:T(128)} %shift_one.1, bf16[3,3,3,128,128]{4,3,2,1,0:T(8,128)(2,1)} %conv_one.1, f32[128]{0:T(128)} %bias_one.1, f32[128]{0:T(128)} %gain_two.1, f32[128]{0:T(128)} %shift_two.1, ...), custom_call_target="tpu_custom_call" | custom-call | tf_op jit(solution)/shard_map/residual_block/pallas_call | solution.py:448
  32.7 0.7 %copy.12 = f32[2,8,48,128]{3,2,1,0:T(8,128)} copy(f32[2,8,48,128]{3,2,1,0:T(8,128)S(1)} %residual_block.1) | data formatting | bytes 786432

commit v6 on v5

--- a/solution.py
+++ b/solution.py
@@ -80,7 +80,7 @@
     below = jnp.minimum(tm, reach)
     above = jnp.minimum(n_tm - 1 - tm, reach)
     barrier = pltpu.get_barrier_semaphore()
-    full, answers, complete = ready.at[0], ready.at[1], ready.at[2]
+    answers, complete = ready.at[0], ready.at[1]
 
     def signal(semaphore, target):
         pl.semaphore_signal(semaphore, inc=1, device_id=target, device_id_type=MESH)
@@ -105,7 +105,7 @@
 
             @pl.when(exists(-d))
             def _(d=d):
-                signal(ready.at[2 + d], device(-d, 0))
+                signal(ready.at[1 + d], device(-d, 0))
 
         @pl.when(jnp.logical_not(hosting))
         def _():
@@ -135,7 +135,7 @@
         )
 
     class Halo:
-        def __init__(self, block, half):
+        def __init__(self, block, half, passed):
             own, prior = pl.ds(count, count), pl.ds(0, count)
             whole, last, head = pl.ds(1, height), pl.ds(height, 1), pl.ds(1, 1)
             above, below = pl.ds(0, 1), pl.ds(height + 1, 1)
@@ -147,7 +147,10 @@
             self.beside = [copy(own, last, own, above, 0, 1), copy(own, head, own, below, 0, -1)]
             halves = [(pl.ds(count + f, 1), pl.ds(f, 1)) for f in range(count)]
             self.onward = [copy(src, whole, dst, whole, 1, 0) for src, dst in halves]
-            self.corners = [copy(own, last, prior, above, 1, 1), copy(own, head, prior, below, 1, -1)]
+            if passed:
+                self.corners = [copy(own, above, prior, above, 1, 0), copy(own, below, prior, below, 1, 0)]
+            else:
+                self.corners = [copy(own, last, prior, above, 1, 1), copy(own, head, prior, below, 1, -1)]
             edge = block.at[:, pl.ds(0, 1)]
             self.all_beside = remote(edge, edge, halo_send.at[half, 0], halo_recv.at[half, 0], 0, 1)
             front = block.at[prior]
@@ -169,8 +172,7 @@
                 for copy in self.corners:
                     copy.start()
 
-        def wait_recv(self):
-            self.all_beside.wait_recv()
+        def wait_onward(self):
             pl.when(exists(-1))(self.all_onward.wait_recv)
 
         def wait_send(self):
@@ -270,7 +272,7 @@
     column = lax.broadcasted_iota(jnp.int32, (cols, width), 0)
 
     def convolved(block, stats, gain, shift, taps):
-        def active(f, i):
+        def active(f, i, moved):
             mean, scale = stats[max(f - count, 0)]
             v = (block[f, i].astype(jnp.float32) - mean) * (scale * gain) + shift
             v = v * (0.5 * jnp.tanh(0.5 * v) + 0.5)
@@ -278,11 +280,21 @@
                 v = jnp.where(row == 0, 0.0, v)
             if i == height + 1:
                 v = jnp.where(row == n_rows - 1, 0.0, v)
+            if moved:
+                moved = jnp.where(column == cols - 1, 0.0, pltpu.roll(v, cols - 1, 0))
+                return v.astype(jnp.bfloat16), moved.astype(jnp.bfloat16)
             return v.astype(jnp.bfloat16)
 
         seen = [[[], [], []] for _ in range(count)]
+        moved = [[], []]
         for i in range(height + 2):
-            a, b, c, d = [active(f, i) for f in range(2 * count)]
+            a, b = active(0, i, False), active(1, i, False)
+            c, d = active(2, i, i >= 2), active(3, i, i >= 2)
+            if i >= 2:
+                c, moved_c = c
+                d, moved_d = d
+                moved[0].append(moved_c)
+                moved[1].append(moved_d)
             b = jnp.where(starts[0] < first, b, c)
             seen[0][0].append(jnp.where(starts[0] < first - 1, a, b))
             seen[0][1].append(b)
@@ -290,20 +302,29 @@
             seen[1][0].append(jnp.where(starts[1] > first, d, b))
             seen[1][1].append(jnp.where(starts[1] > first, d, c))
             seen[1][2].append(d)
-        right = taps[...].reshape(9 * width, 3 * width)
+        right = taps[...].reshape(9 * width, 3 * width)[: 8 * width]
+        ninth = taps[2, 2]
+        blank = jnp.zeros((width, width), jnp.bfloat16)
+        ninth = jnp.concatenate(
+            [ninth[:, : 2 * width], jnp.concatenate([blank, ninth[:, 2 * width :]], axis=1)], axis=0
+        )
         results = []
         for f in range(count):
             pieces = [
                 jnp.concatenate(seen[f][dt][dy : dy + height], axis=0) for dt in range(3) for dy in range(3)
             ]
-            wide = jnp.dot(jnp.concatenate(pieces, axis=1), right, preferred_element_type=jnp.float32)
+            wide = jnp.dot(jnp.concatenate(pieces[:8], axis=1), right, preferred_element_type=jnp.float32)
+            last = jnp.concatenate([pieces[8], jnp.concatenate(moved[f], axis=0)], axis=1)
+            last = jnp.dot(last, ninth, preferred_element_type=jnp.float32)
             rows = []
             for i in range(height):
                 y = wide[i * cols : (i + 1) * cols]
-                before = pltpu.roll(y[:, :width], 1, 0)
+                z = last[i * cols : (i + 1) * cols]
+                before = pltpu.roll(y[:, :width] + z[:, :width], 1, 0)
                 after = pltpu.roll(y[:, 2 * width :], cols - 1, 0)
                 rows.append(
                     y[:, width : 2 * width]
+                    + z[:, width:]
                     + jnp.where(column == 0, 0.0, before)
                     + jnp.where(column == cols - 1, 0.0, after)
                 )
@@ -330,14 +351,14 @@
             stats.append((mean, lax.rsqrt(var + 1e-6)))
         return stats
 
+    await_signals(barrier, announced)
+    answer()
     load_frames.wait()
     tms_one[pl.ds(0, 1)] = local_stats(
         [[raw[count + f, 1 + i] for i in range(height)] for f in range(count)]
     )
-    await_signals(barrier, announced)
     tm_sums = Frames(tms_one, 0)
     tm_sums.start(-1)
-    answer()
 
     load_lens.wait()
     starts, stops = [], []
@@ -362,12 +383,12 @@
     known = slot <= len(offsets)
     inside = [known & (frame >= starts[f]) & (frame < stops[f]) for f in range(count)]
 
-    halo_one = Halo(raw, 0)
+    halo_one = Halo(raw, 0, passed=True)
     for d in range(1, reach + 1):
 
         @pl.when(exists(d))
         def _(d=d):
-            pl.semaphore_wait(ready.at[2 + d], 1)
+            pl.semaphore_wait(ready.at[1 + d], 1)
             tm_sums.copies[d].start()
 
         if d == reach // 2:
@@ -385,25 +406,17 @@
     def _():
         pl.semaphore_wait(complete, 1)
 
-    @pl.when(exists(-1))
-    def _():
-        signal(full, device(-1, 0))
-
+    halo_one.start_beside()
     tm_sums.wait_recv()
     rows_one[pl.ds(0, 1)] = video_sums(tms_one, inside, entries)
     row_sums = Rows(rows_one, 0)
     row_sums.start()
-    halo_one.start_beside()
-
-    @pl.when(exists(1))
-    def _():
-        pl.semaphore_wait(full, 1)
-
+    halo_one.all_beside.wait_recv()
     halo_one.start_corners()
     load_vecs.wait()
     row_sums.all.wait_recv()
     stats = video_stats(rows_one, entries)
-    halo_one.wait_recv()
+    halo_one.wait_onward()
     load_one.wait()
     results = convolved(raw, stats, vecs[0:1], vecs[1:2], taps_one)
     results = [[(y + vecs[2:3]).astype(jnp.bfloat16) for y in rows] for rows in results]
@@ -413,7 +426,7 @@
     rows_two[pl.ds(0, 1)] = local_stats(results)
     row_sums_two = Rows(rows_two, 1)
     row_sums_two.start()
-    halo_two = Halo(mid, 1)
+    halo_two = Halo(mid, 1, passed=False)
     halo_two.start_beside()
     halo_two.start_corners()
     halo_two.start_onward(0, 1)
@@ -427,7 +440,8 @@
     tm_sums_two.start(-1, 1)
     tm_sums_two.wait_recv()
     stats = frame_stats(tms_two, inside, entries)
-    halo_two.wait_recv()
+    halo_two.all_beside.wait_recv()
+    halo_two.wait_onward()
     load_two.wait()
     results = convolved(mid, stats, vecs[3:4], vecs[4:5], taps_two)
     for f in range(count):
@@ -458,7 +472,7 @@
             pltpu.VMEM((n_rows, width), jnp.float32),
             pltpu.VMEM((window, width), jnp.float32),
             pltpu.VMEM((window, width), jnp.float32),
-            pltpu.SemaphoreType.REGULAR((3 + near // 2 + 1,)),
+            pltpu.SemaphoreType.REGULAR((2 + near // 2,)),
             pltpu.SemaphoreType.DMA((5,)),
             pltpu.SemaphoreType.DMA((2, 2)),
             pltpu.SemaphoreType.DMA((2, 2)),

time: 33.6 us -> 32.8 us (0.976)
  Pallas kernels: 32.7 us -> 32 us
    pallas_call x1, Pallas kernels: 32.7 us -> 32 us  [per_device(): pl.pallas_call(functools.partial(kernel, n_tm, n_rows), out_shape=pltpu.V...]
where the time goes in v6:
time: 32.8 us; the launch traced here: 32.7 us
  Pallas kernels  32 us (98%)
  local copies, waits for them, and re-layouts  0.75 us (2%)
    pallas_call x1, Pallas kernels, per_device(): pl.pallas_call(functools.partial(kernel, n_tm, n_rows), out_shape=pltpu.V...  32 us
    unnamed x1, local copies, waits for them, and re-layouts  0.75 us

profile of v6, /device:TPU:128, one launch (start us, length us, event | category | flops | bytes accessed | tf_op | source)
XLA Modules:
  0.0 32.7 jit_solution(2156225261488537056)
XLA Ops:
  0.0 32.0 %residual_block.1 = f32[2,8,48,128]{3,2,1,0:T(8,128)S(1)} custom-call(bf16[2,8,48,128]{3,2,1,0:T(8,128)(2,1)} %frames.1, s32[8]{0:T(128)} %lengths.1, f32[128]{0:T(128)} %gain_one.1, f32[128]{0:T(128)} %shift_one.1, bf16[3,3,3,128,128]{4,3,2,1,0:T(8,128)(2,1)} %conv_one.1, f32[128]{0:T(128)} %bias_one.1, f32[128]{0:T(128)} %gain_two.1, f32[128]{0:T(128)} %shift_two.1, ...), custom_call_target="tpu_custom_call" | custom-call | tf_op jit(solution)/shard_map/residual_block/pallas_call | solution.py:462
  32.0 0.7 %copy.12 = f32[2,8,48,128]{3,2,1,0:T(8,128)} copy(f32[2,8,48,128]{3,2,1,0:T(8,128)S(1)} %residual_block.1) | data formatting | bytes 786432

commit v7 on v6

--- a/solution.py
+++ b/solution.py
@@ -243,13 +243,13 @@
             squares.append(group_total(square, place))
         return by_place(place, totals + squares)
 
-    def video_sums(slots, inside, entries):
+    def video_sums(slots, inside, shares):
         parts = slots[...]
         merged = []
         for f in range(count):
             total = jnp.sum(jnp.where(inside[f], parts, 0.0), axis=0, keepdims=True)
             total = total + jnp.where(odd, pltpu.roll(total, 1, 1), pltpu.roll(total, width - 1, 1))
-            off = parts * (1.0 / per_block) - total * (1.0 / entries[f])
+            off = parts * (1.0 / per_block) - total * shares[f]
             between = jnp.sum(jnp.where(inside[f], off * off, 0.0), axis=0, keepdims=True) * per_block
             between = pltpu.roll(between, 2, 1) + jnp.where(
                 odd, pltpu.roll(between, 3, 1), pltpu.roll(between, 1, 1)
@@ -257,14 +257,13 @@
             merged.append(total + jnp.where(head, 0.0, between))
         return jnp.where(odd, merged[1], merged[0])
 
-    def video_stats(slots, entries):
+    def video_stats(slots, held, share):
         parts = slots[...]
-        share = jnp.where(odd, entries[1], entries[0])
         total = jnp.sum(parts, axis=0, keepdims=True)
-        mean = total / (share * n_rows)
-        off = parts * (1.0 / share) - mean
-        between = jnp.sum(off * off, axis=0, keepdims=True) * share
-        var = (total + pltpu.roll(between, 2, 1)) / (share * n_rows)
+        mean = total * share * (1.0 / n_rows)
+        off = parts * share - mean
+        between = jnp.sum(off * off, axis=0, keepdims=True) * held
+        var = (total + pltpu.roll(between, 2, 1)) * share * (1.0 / n_rows)
         near = neighbours(jnp.where(head, mean, lax.rsqrt(var + 1e-6)))
         spread = [by_place(place, [near[i - k] for i in range(4)]) for k in range(4)]
         return [(spread[f], spread[count + f]) for f in range(count)]
@@ -338,16 +337,16 @@
         between = jnp.sum(off * off, axis=0, keepdims=True) * per_block
         return total + jnp.where(head, 0.0, pltpu.roll(between, 2, 1))
 
-    def frame_stats(slots, inside, entries):
+    def frame_stats(slots, inside, shares):
         parts = slots[...]
         per_frame = per_block * n_rows
         stats = []
         for f in range(count):
             total = jnp.sum(jnp.where(inside[f], parts, 0.0), axis=0, keepdims=True)
-            mean = group_total(jnp.where(head, total, 0.0), place) / (entries[f] * n_rows)
+            mean = group_total(jnp.where(head, total, 0.0), place) * (shares[f] * (1.0 / n_rows))
             off = parts * (1.0 / per_frame) - mean
             between = jnp.sum(jnp.where(inside[f], off * off, 0.0), axis=0, keepdims=True) * per_frame
-            var = group_total(jnp.where(head, between, total), place) / (entries[f] * n_rows)
+            var = group_total(jnp.where(head, between, total), place) * (shares[f] * (1.0 / n_rows))
             stats.append((mean, lax.rsqrt(var + 1e-6)))
         return stats
 
@@ -375,6 +374,9 @@
         starts.append(start)
         stops.append(stop)
     entries = [(stops[f] - starts[f]).astype(jnp.float32) * per_block for f in range(count)]
+    shares = [1.0 / jnp.full((1, width), entries[f], jnp.float32) for f in range(count)]
+    held = jnp.where(odd, entries[1], entries[0])
+    share = jnp.where(odd, shares[1], shares[0])
     slot = lax.broadcasted_iota(jnp.int32, tms_one.shape, 0)
     lane = lax.broadcasted_iota(jnp.int32, tms_one.shape, 1)
     far = (slot + 1) // 2
@@ -408,14 +410,14 @@
 
     halo_one.start_beside()
     tm_sums.wait_recv()
-    rows_one[pl.ds(0, 1)] = video_sums(tms_one, inside, entries)
+    rows_one[pl.ds(0, 1)] = video_sums(tms_one, inside, shares)
     row_sums = Rows(rows_one, 0)
     row_sums.start()
     halo_one.all_beside.wait_recv()
     halo_one.start_corners()
     load_vecs.wait()
     row_sums.all.wait_recv()
-    stats = video_stats(rows_one, entries)
+    stats = video_stats(rows_one, held, share)
     halo_one.wait_onward()
     load_one.wait()
     results = convolved(raw, stats, vecs[0:1], vecs[1:2], taps_one)
@@ -439,7 +441,7 @@
     tm_sums_two = Frames(tms_two, 1)
     tm_sums_two.start(-1, 1)
     tm_sums_two.wait_recv()
-    stats = frame_stats(tms_two, inside, entries)
+    stats = frame_stats(tms_two, inside, shares)
     halo_two.all_beside.wait_recv()
     halo_two.wait_onward()
     load_two.wait()

time: 32.8 us -> 32.8 us (level)
  no operation moved by 1% of the time
where the time goes in v7:
time: 32.8 us; the launch traced here: 32.7 us
  Pallas kernels  32 us (98%)
  local copies, waits for them, and re-layouts  0.75 us (2%)
    pallas_call x1, Pallas kernels, per_device(): pl.pallas_call(functools.partial(kernel, n_tm, n_rows), out_shape=pltpu.V...  32 us
    unnamed x1, local copies, waits for them, and re-layouts  0.75 us

profile of v7, /device:TPU:128, one launch (start us, length us, event | category | flops | bytes accessed | tf_op | source)
XLA Modules:
  0.0 32.7 jit_solution(13576188401588001299)
XLA Ops:
  0.0 32.0 %residual_block.1 = f32[2,8,48,128]{3,2,1,0:T(8,128)S(1)} custom-call(bf16[2,8,48,128]{3,2,1,0:T(8,128)(2,1)} %frames.1, s32[8]{0:T(128)} %lengths.1, f32[128]{0:T(128)} %gain_one.1, f32[128]{0:T(128)} %shift_one.1, bf16[3,3,3,128,128]{4,3,2,1,0:T(8,128)(2,1)} %conv_one.1, f32[128]{0:T(128)} %bias_one.1, f32[128]{0:T(128)} %gain_two.1, f32[128]{0:T(128)} %shift_two.1, ...), custom_call_target="tpu_custom_call" | custom-call | tf_op jit(solution)/shard_map/residual_block/pallas_call | solution.py:464
  32.0 0.7 %copy.12 = f32[2,8,48,128]{3,2,1,0:T(8,128)} copy(f32[2,8,48,128]{3,2,1,0:T(8,128)S(1)} %residual_block.1) | data formatting | bytes 786432

commit v8 on v7

--- a/solution.py
+++ b/solution.py
@@ -439,7 +439,8 @@
     row_sums_two.all.wait_recv()
     tms_two[pl.ds(0, 1)] = frame_sums(rows_two)
     tm_sums_two = Frames(tms_two, 1)
-    tm_sums_two.start(-1, 1)
+    tm_sums_two.start(-1)
+    tm_sums_two.start(1)
     tm_sums_two.wait_recv()
     stats = frame_stats(tms_two, inside, shares)
     halo_two.all_beside.wait_recv()

time: 32.8 us -> 32.8 us (level)
  no operation moved by 1% of the time
where the time goes in v8:
time: 32.8 us; the launch traced here: 32.7 us
  Pallas kernels  32 us (98%)
  local copies, waits for them, and re-layouts  0.75 us (2%)
    pallas_call x1, Pallas kernels, per_device(): pl.pallas_call(functools.partial(kernel, n_tm, n_rows), out_shape=pltpu.V...  32 us
    unnamed x1, local copies, waits for them, and re-layouts  0.75 us

profile of v8, /device:TPU:128, one launch (start us, length us, event | category | flops | bytes accessed | tf_op | source)
XLA Modules:
  0.0 32.7 jit_solution(12946920979647410069)
XLA Ops:
  0.0 32.0 %residual_block.1 = f32[2,8,48,128]{3,2,1,0:T(8,128)S(1)} custom-call(bf16[2,8,48,128]{3,2,1,0:T(8,128)(2,1)} %frames.1, s32[8]{0:T(128)} %lengths.1, f32[128]{0:T(128)} %gain_one.1, f32[128]{0:T(128)} %shift_one.1, bf16[3,3,3,128,128]{4,3,2,1,0:T(8,128)(2,1)} %conv_one.1, f32[128]{0:T(128)} %bias_one.1, f32[128]{0:T(128)} %gain_two.1, f32[128]{0:T(128)} %shift_two.1, ...), custom_call_target="tpu_custom_call" | custom-call | tf_op jit(solution)/shard_map/residual_block/pallas_call | solution.py:465
  32.0 0.7 %copy.12 = f32[2,8,48,128]{3,2,1,0:T(8,128)} copy(f32[2,8,48,128]{3,2,1,0:T(8,128)S(1)} %residual_block.1) | data formatting | bytes 786432

commit v9 on v8

--- a/solution.py
+++ b/solution.py
@@ -15,10 +15,6 @@
 def tm_offsets(n_tm, count):
     reach = min(-(-(MOST - 1) // count), n_tm - 1)
     return [d for far in range(1, reach + 1) for d in (far, -far)]
-
-
-def tm_hops(d):
-    return abs(d) // 4 + min(abs(d) % 4, 4 - abs(d) % 4)
 
 
 def wrapped(index, offset, size):
@@ -101,7 +97,7 @@
     announced = below + jnp.where(hosting, 0, 1)
 
     def answer():
-        for d in range(1, reach + 1):
+        for d in range(reach, 0, -1):
 
             @pl.when(exists(-d))
             def _(d=d):
@@ -205,7 +201,7 @@
                 self.all[n] = remote(others, others, *sems, 0, 1)
 
         def start(self, *signs):
-            for d in sorted(range(1, reach + 1), key=lambda d: -tm_hops(d)):
+            for d in range(reach, 0, -1):
                 for sign in signs:
                     pl.when(exists(sign * d))(self.copies[sign * d].start)
 

time: 32.8 us -> 32.8 us (level)
  no operation moved by 1% of the time
where the time goes in v9:
time: 32.8 us; the launch traced here: 32.7 us
  Pallas kernels  31.9 us (97%)
  local copies, waits for them, and re-layouts  0.75 us (2%)
    pallas_call x1, Pallas kernels, per_device(): pl.pallas_call(functools.partial(kernel, n_tm, n_rows), out_shape=pltpu.V...  31.9 us
    unnamed x1, local copies, waits for them, and re-layouts  0.75 us

profile of v9, /device:TPU:128, one launch (start us, length us, event | category | flops | bytes accessed | tf_op | source)
XLA Modules:
  0.0 32.7 jit_solution(15619176140551901683)
XLA Ops:
  0.0 31.9 %residual_block.1 = f32[2,8,48,128]{3,2,1,0:T(8,128)S(1)} custom-call(bf16[2,8,48,128]{3,2,1,0:T(8,128)(2,1)} %frames.1, s32[8]{0:T(128)} %lengths.1, f32[128]{0:T(128)} %gain_one.1, f32[128]{0:T(128)} %shift_one.1, bf16[3,3,3,128,128]{4,3,2,1,0:T(8,128)(2,1)} %conv_one.1, f32[128]{0:T(128)} %bias_one.1, f32[128]{0:T(128)} %gain_two.1, f32[128]{0:T(128)} %shift_two.1, ...), custom_call_target="tpu_custom_call" | custom-call | tf_op jit(solution)/shard_map/residual_block/pallas_call | solution.py:461
  32.0 0.7 %copy.12 = f32[2,8,48,128]{3,2,1,0:T(8,128)} copy(f32[2,8,48,128]{3,2,1,0:T(8,128)S(1)} %residual_block.1) | data formatting | bytes 786432

commit v10 on v8

--- a/solution.py
+++ b/solution.py
@@ -101,7 +101,7 @@
     announced = below + jnp.where(hosting, 0, 1)
 
     def answer():
-        for d in range(1, reach + 1):
+        for d in range(reach, 0, -1):
 
             @pl.when(exists(-d))
             def _(d=d):

time: 32.8 us -> 32.8 us (level)
  no operation moved by 1% of the time
where the time goes in v10:
time: 32.8 us; the launch traced here: 32.7 us
  Pallas kernels  32 us (98%)
  local copies, waits for them, and re-layouts  0.75 us (2%)
    pallas_call x1, Pallas kernels, per_device(): pl.pallas_call(functools.partial(kernel, n_tm, n_rows), out_shape=pltpu.V...  32 us
    unnamed x1, local copies, waits for them, and re-layouts  0.75 us

profile of v10, /device:TPU:128, one launch (start us, length us, event | category | flops | bytes accessed | tf_op | source)
XLA Modules:
  0.0 32.7 jit_solution(15615468679816830051)
XLA Ops:
  0.0 32.0 %residual_block.1 = f32[2,8,48,128]{3,2,1,0:T(8,128)S(1)} custom-call(bf16[2,8,48,128]{3,2,1,0:T(8,128)(2,1)} %frames.1, s32[8]{0:T(128)} %lengths.1, f32[128]{0:T(128)} %gain_one.1, f32[128]{0:T(128)} %shift_one.1, bf16[3,3,3,128,128]{4,3,2,1,0:T(8,128)(2,1)} %conv_one.1, f32[128]{0:T(128)} %bias_one.1, f32[128]{0:T(128)} %gain_two.1, f32[128]{0:T(128)} %shift_two.1, ...), custom_call_target="tpu_custom_call" | custom-call | tf_op jit(solution)/shard_map/residual_block/pallas_call | solution.py:465
  32.0 0.7 %copy.12 = f32[2,8,48,128]{3,2,1,0:T(8,128)} copy(f32[2,8,48,128]{3,2,1,0:T(8,128)S(1)} %residual_block.1) | data formatting | bytes 786432
